TPU v7x, 32 devices: a whole 2x2x4 slice. The times are simulated.
32 devices in a mesh: patch: 8 (over z, y), dp: 4 (over x, core).
Axes of the slice: x: 2, y: 2, z: 4, core: 2. Of those that a mesh axis runs over, the one named last changes fastest.
Arguments:
- grid: bfloat16 [8, 16384, 264], P('dp', 'patch'), may hold values from -6 to 6
- targets: float32 [8, 16384, 84], P('dp', 'patch'), may hold values from -6 to 6
- area: float32 [16384], P('patch'), may hold values from 0.1 to 1
- sigma_weight: float32 [8], P('dp'), may hold values from 0.5 to 2
- level_weight: float32 [84], replicated, may hold values from 0.2 to 2
- valid: int32 [8, 16384], P('dp', 'patch'), may hold values from 0 to 1
- enc_index: int32 [4096, 4], P('patch'), may hold values from 0 to 2047
- dec_index: int32 [16384, 3], P('patch'), may hold values from 0 to 511
- neighbours: int32 [4096, 16], P('patch'), may hold values from 0 to 575, as said below
- params: float32 [3325440], P(('patch', 'dp'))
- first_moment: float32 [3325440], P(('patch', 'dp'))
- second_moment: float32 [3325440], P(('patch', 'dp')), as said below
- average: float32 [3325440], P(('patch', 'dp'))
Outputs:
- loss_pair: float32 [2], replicated
- norms: float32 [2, 7], replicated
- new_params: float32 [3325440], P(('patch', 'dp'))
- new_first: float32 [3325440], P(('patch', 'dp'))
- new_second: float32 [3325440], P(('patch', 'dp'))
- new_average: float32 [3325440], P(('patch', 'dp'))
Inputs may be any that keep to these rules, and one draw needn't show every extreme that they name: `neighbours`: entries below 32 name the lower adjacent patch's last 32 rows, entries of 544 or more the upper one's first 32 rows, the others the patch's own rows; every rim row of both sides is read by some node of every patch; the patches close into a loop. `second_moment`: second moments are positive.
All inputs are finite; a program needn't handle non-finite values.
Results may differ from a plain program's by a relative error of at most 0.0025.
The roundings to bfloat16 on the way count: a program that leaves them out, or rounds other values in their place, can miss the bound.
Values may be sent and summed in bfloat16 or wider, within the bound.
No kernel may reach another device: no remote copies, remote signals or barrier semaphores. Data moves between devices by JAX's collectives and lax.ppermute only.
A program may use at most 320 MiB of HBM per device.

v0:
```python
import functools
import math

import jax
import jax.numpy as jnp
from jax import lax
from jax.experimental import pallas as pl
from jax.experimental.pallas import tpu as pltpu
from jax.sharding import PartitionSpec as P

D = 512
HEADS = 4
HEAD_DIM = 128
FF = 2048
C_OUT = 84
C_IN = 264
STEP = 10
EPS_NORM = 1e-05
BETA_ONE = 0.9
BETA_TWO = 0.999
LAMB_EPS = 1e-06
DECAY = 0.01
RATE = 0.2
EMA_KEEP = 0.8
BF = jnp.bfloat16
F32 = jnp.float32
SCALE = HEAD_DIM ** (-0.5)
LOG2E = 1.4426950408889634
ABSENT = -1e30
CP = 96
AXES = ("patch", "dp")

LEAD = 8
ROW_ENC = LEAD
ROW_QKV = ROW_ENC + C_IN
ROW_OUT = ROW_QKV + 3 * D
ROW_UP = ROW_OUT + D
ROW_DOWN = ROW_UP + 4 * D
ROW_DEC = ROW_DOWN + FF
ROW_GAIN = ROW_DEC + C_OUT
ROW_END = ROW_GAIN + 3
ROWS_ALL = -(-ROW_END // 16) * 16


def matrix_shapes():
    return [(C_IN, D), (D, 3 * D), (D, D), (D, FF), (FF, D), (D, C_OUT), (3, D)]


def segment_bounds():
    bounds = []
    offset = 0
    for row_count, col_count in matrix_shapes():
        bounds.append((offset, offset + row_count * col_count))
        offset += row_count * col_count
    return bounds


NPARAM_USED = segment_bounds()[-1][1]


def dot(a, b):
    return lax.dot_general(a, b, (((1,), (0,)), ((), ())), preferred_element_type=F32)


def dot_nt(a, b):
    return lax.dot_general(a, b, (((1,), (1,)), ((), ())), preferred_element_type=F32)


def dot_tn(a, b):
    return lax.dot_general(a, b, (((0,), (0,)), ((), ())), preferred_element_type=F32)


def split(x):
    high = x.astype(BF)
    return high, (x - high.astype(F32)).astype(BF)


def sigmoid(x):
    return 0.5 * jnp.tanh(0.5 * x) + 0.5


def slope(x, s):
    return s * (1.0 + x * (1.0 - s))


def norm(x):
    c = x - jnp.mean(x, -1, keepdims=True)
    r = lax.rsqrt(jnp.mean(c * c, -1, keepdims=True) + EPS_NORM)
    return c * r, r


def norm_back(grad, gain, hat, r):
    g = grad * gain
    return r * (
        g
        - jnp.mean(g, -1, keepdims=True)
        - hat * jnp.mean(g * hat, -1, keepdims=True)
    )


def put_flat(ref, value, first, period):
    for lane in range(D // 128):
        ref[pl.ds(first + lane, value.shape[0], stride=period), :] = value[
            :, lane * 128 : lane * 128 + 128
        ]


def kernel_call(body, out_shape, scratch=(), flops=0, nbytes=0):
    return pl.pallas_call(
        body,
        out_shape=out_shape,
        scratch_shapes=list(scratch),
        compiler_params=pltpu.CompilerParams(vmem_limit_bytes=58 << 20),
        cost_estimate=pl.CostEstimate(flops=flops, bytes_accessed=nbytes, transcendentals=0),
    )


def shape(dims, dtype=F32):
    return jax.ShapeDtypeStruct(tuple(dims), dtype)


def count_rows(index_t, base, rows, cols):
    ids = lax.broadcasted_iota(jnp.int32, (rows, cols), 0) + base
    total = jnp.zeros((rows, cols), F32)
    for k in range(index_t.shape[0]):
        total = total + jnp.where(index_t[k : k + 1, :] == ids, 1.0, 0.0)
    return total


def count_encoder_body(enc, enc_t, enc_m, enc_mt):
    nodes, pixels = enc_m.shape

    @pl.loop(0, nodes // 32)
    def _(i):
        rows = pl.ds(pl.multiple_of(i * 32, 32), 32)
        index = enc[rows, :]
        ids = lax.broadcasted_iota(jnp.int32, (32, pixels), 1)
        total = jnp.zeros((32, pixels), F32)
        for k in range(index.shape[1]):
            total = total + jnp.where(index[:, k : k + 1] == ids, 1.0, 0.0)
        enc_m[rows, :] = total.astype(BF)

    @pl.loop(0, pixels // 64)
    def _(i):
        rows = pl.ds(pl.multiple_of(i * 64, 64), 64)
        enc_mt[rows, :] = count_rows(enc_t, i * 64, 64, nodes).astype(BF)


def count_rest_body(dec_t, nbr_t, targets, dec_mt, log_c, targets_t):
    nodes, pixels = dec_mt.shape

    @pl.loop(0, nodes // 32)
    def _(i):
        rows = pl.ds(pl.multiple_of(i * 32, 32), 32)
        dec_mt[rows, :] = count_rows(dec_t, i * 32, 32, pixels).astype(BF)

    @pl.loop(0, log_c.shape[0] // 64)
    def _(i):
        rows = pl.ds(pl.multiple_of(i * 64, 64), 64)
        total = count_rows(nbr_t, i * 64, 64, nodes)
        log_c[rows, :] = jnp.where(total > 0.0, jnp.log2(jnp.maximum(total, 1.0)), ABSENT)

    targets_t[...] = jnp.zeros(targets_t.shape, F32)
    for s in range(targets.shape[0]):

        @pl.loop(0, pixels // 256)
        def _(i):
            part = pl.ds(pl.multiple_of(i * 256, 256), 256)
            targets_t[s, 0:C_OUT, part] = targets[s, part, :].T


def count_encoder(enc_index, pixels):
    nodes = enc_index.shape[0]
    return kernel_call(
        count_encoder_body,
        [shape((nodes, pixels), BF), shape((pixels, nodes), BF)],
        nbytes=5 << 20,
        flops=1 << 29,
    )(enc_index, enc_index.T)


def count_rest(dec_index, neighbours, targets):
    nodes, pixels = neighbours.shape[0], dec_index.shape[0]
    ext = nodes + 2 * (nodes // 16)
    return kernel_call(
        count_rest_body,
        [shape((nodes, pixels), BF), shape((ext, nodes)), shape((targets.shape[0], CP, pixels))],
        nbytes=8 << 20,
        flops=1 << 29,
    )(dec_index.T, neighbours.T, targets)


def tile_sources(starts, rows):
    return [
        [(d, tile * 16 - s) for d, s in enumerate(starts) if s <= tile * 16 < s + rows]
        for tile in range(ROWS_ALL // 16)
    ]


def assemble(read, window_rows, sources, first_row, rows, put):
    tile, last = first_row // 16, (first_row + rows) // 16
    while tile < last:
        source = sources[tile]
        if len(source) == 1:
            count = 1
            while (
                tile + count < last
                and len(sources[tile + count]) == 1
                and sources[tile + count][0][0] == source[0][0]
                and count < 8
            ):
                count += 1
            d, off = source[0]
            value = read(d, off, 16 * count)
        else:
            count = 1
            value = None
            for d, off in source:
                part = read(d, off, 16).astype(F32)
                if off + 16 == window_rows:
                    part = jnp.where(
                        lax.broadcasted_iota(jnp.int32, part.shape, 0) < 15, part, 0.0
                    )
                value = part if value is None else value + part
            value = value.astype(BF)
        put(tile * 16 - first_row, value)
        tile += count


def wide(stage, ref, period):
    for lane in range(D // 128):
        for c in range(period):
            lanes = slice(c * D + lane * 128, c * D + lane * 128 + 128)
            ref[:, lanes] = stage[lane, pl.ds(c, ref.shape[0], stride=period), :].astype(BF)


def unpack_body(plan, parts, sources, place_of, count, *refs):
    me, pieces, refs = refs[0], refs[1 : count + 1], refs[count + 1 :]
    outs, (windows, stage, sems) = refs[: len(parts)], refs[len(parts) :]
    copies = []

    for k, (piece, at, slot, first, rows) in enumerate(plan):
        copy = pltpu.make_async_copy(
            pieces[piece].at[pl.ds(at, rows), :],
            windows.at[slot, pl.ds(first, rows), :],
            sems.at[k],
        )
        copy.start()
        copies.append(copy)
    for copy in copies:
        copy.wait()
    here = me[0]
    window_rows = windows.shape[1]

    def read(d, off, rows):
        return windows[place_of(here, d), off : off + rows, :]

    for part, ref in zip(parts, outs):
        if part == "count":
            total = jnp.sum(windows[:, window_rows - 16 :, 0:128].astype(F32), axis=0)[15:16, :]
            lanes = lax.broadcasted_iota(jnp.int32, (1, 128), 1)
            digits = jnp.where(lanes == 0, 128.0, jnp.where(lanes == 1, 1.0, 0.0)) * total
            ref[...] = jnp.sum(digits, axis=1, keepdims=True) + jnp.zeros((8, 128), F32)
            continue
        first, rows, period, _ = PARTS[part]

        def direct(off, value):
            ref[off : off + value.shape[0], :] = value

        def staged(off, value):
            wide_value = value.astype(F32)
            for lane in range(D // 128):
                stage[lane, off : off + value.shape[0], :] = wide_value[
                    :, lane * 128 : lane * 128 + 128
                ]

        if part == "gain":
            assemble(read, window_rows, sources, first, rows, staged)
            row = ROW_GAIN - first
            for lane in range(D // 128):
                ref[:, lane * 128 : lane * 128 + 128] = stage[lane, row : row + 1, :] + jnp.zeros(
                    (8, 128), F32
                )
        elif period == 1:
            assemble(read, window_rows, sources, first, rows, direct)
        else:
            assemble(read, window_rows, sources, first, rows, staged)
            if part == "enc":
                for lane in range(D // 128):
                    lanes = slice(lane * 128, lane * 128 + 128)
                    ref[:, lanes] = stage[lane, LEAD:ROW_QKV, :].astype(BF)
            else:
                wide(stage, ref, period)


PARTS = {
    "enc": (0, ROW_QKV, 0, (C_IN, D)),
    "qkv": (ROW_QKV, 3 * D, 3, (D, 3 * D)),
    "gain": (ROW_GAIN // 16 * 16, 16, 0, (8, D)),
    "out": (ROW_OUT, D, 1, (D, D)),
    "up": (ROW_UP, 4 * D, 4, (D, FF)),
    "down": (ROW_DOWN, FF, 1, (FF, D)),
    "tail": (ROW_DEC, ROWS_ALL - ROW_DEC, 1, (ROWS_ALL - ROW_DEC, D)),
}


def unpack(me, pieces, plan, parts, place_of, slots, rows, starts):
    sources = tile_sources(starts, rows)
    outs = [
        shape((8, 128)) if p == "count" else shape(PARTS[p][3], F32 if p == "gain" else BF)
        for p in parts
    ]
    return pl.pallas_call(
        functools.partial(unpack_body, plan, parts, sources, place_of, len(pieces)),
        out_shape=outs,
        in_specs=[pl.BlockSpec(memory_space=pltpu.SMEM)]
        + [pl.BlockSpec(memory_space=pl.ANY)] * len(pieces),
        scratch_shapes=[
            pltpu.VMEM((slots, rows, D), BF),
            pltpu.VMEM((D // 128, 4 * D, 128), F32),
            pltpu.SemaphoreType.DMA((len(plan),)),
        ],
        compiler_params=pltpu.CompilerParams(vmem_limit_bytes=58 << 20),
        cost_estimate=pl.CostEstimate(
            flops=0, bytes_accessed=slots * rows * D * 4, transcendentals=0
        ),
    )(me, *pieces)


def permute(x, mask):
    count = lax.axis_size(AXES)
    return lax.ppermute(x, AXES, [(d, d ^ mask) for d in range(count)])


def place_by_xor(here, d):
    return jnp.bitwise_xor(here, d)


def gather_windows(window, first_work, second_work):
    rows = window.shape[0]
    half = rows // 2
    pieces, plan = [], []

    def add(piece, near, parts):
        for part, flip in ((piece, 0), (permute(piece, 1), 1)):
            for at, slot, to, size in parts:
                plan.append((len(pieces), at, slot ^ near ^ flip, to, size))
            pieces.append(part)

    planes = (8, 16, 24)
    others = [permute(window, m) for m in planes]
    by_x, by_y = permute(window, 2), permute(window, 4)
    first_done = first_work()
    others, by_x, by_y, first_done = lax.optimization_barrier(
        (jnp.concatenate(others), by_x, by_y, first_done)
    )
    others_x, others_y = permute(others, 2), permute(others, 4)
    second_done = second_work()
    others_x, others_y, second_done = lax.optimization_barrier((others_x, others_y, second_done))

    def halves(near_part, far_part, first):
        far = [far_part[i * rows + first : i * rows + first + half] for i in range(3)]
        return jnp.concatenate([near_part[first : first + half]] + far)

    across_a = permute(halves(by_y, others_y, 0), 2)
    across_b = permute(halves(by_x, others_x, half), 4)
    whole = [(0, 0, 0, rows)]
    stacked = [(i * rows, slot, 0, rows) for i, slot in enumerate(planes)]
    add(window, 0, whole)
    add(by_x, 2, whole)
    add(by_y, 4, whole)
    add(others, 0, stacked)
    add(others_x, 2, stacked)
    add(others_y, 4, stacked)
    add(across_a, 6, [(i * half, slot, 0, half) for i, slot in enumerate((0,) + planes)])
    add(across_b, 6, [(i * half, slot, half, half) for i, slot in enumerate((0,) + planes)])
    return pieces, plan, first_done, second_done


def encode_body(grid, w_enc, enc_m, w_qkv, gains, h0, qkv, high, low):
    samples, pixels = grid.shape[0], grid.shape[2]
    nodes = h0.shape[1]
    for s in range(samples):

        @pl.loop(0, pixels // 512, unroll=True)
        def _(i):
            rows = pl.ds(pl.multiple_of(i * 512, 512), 512)
            pre = dot_tn(grid[s, :, rows], w_enc[...])
            value = pre * sigmoid(pre)
            high[rows, :], low[rows, :] = split(value)

        @pl.loop(0, nodes // 512, unroll=True)
        def _(i):
            rows = pl.ds(pl.multiple_of(i * 512, 512), 512)
            counts = enc_m[rows, :]
            start = (dot(counts, high[...]) + dot(counts, low[...])) * 0.25
            h0[s, rows, :] = start
            hat, _ = norm(start)
            n1 = (hat * gains[0:1, :]).astype(BF)
            qkv[s, rows, :] = dot(n1, w_qkv[...]).astype(BF)


def encode(grid, w_enc, enc_m, w_qkv, gains):
    samples, pixels = grid.shape[0], grid.shape[2]
    nodes = enc_m.shape[0]
    return kernel_call(
        encode_body,
        [shape((samples, nodes, D)), shape((samples, nodes, 3 * D), BF)],
        [pltpu.VMEM((pixels, D), BF), pltpu.VMEM((pixels, D), BF)],
        nbytes=12 << 20,
        flops=8 << 30,
    )(grid, w_enc, enc_m, w_qkv, gains)


def gather_pairs(qkv, before, after, pairs, s):
    halo, nodes = before.shape[1], qkv.shape[1]
    pairs[0:halo, :] = before[s]
    pairs[halo : halo + nodes, :] = qkv[s, :, D:]
    pairs[halo + nodes :, :] = after[s]


def attention_weights(keys, query, log_c):
    x = dot_nt(keys, query) * (SCALE * LOG2E) + log_c[...]
    e = jnp.exp2(x - jnp.max(x, 0, keepdims=True))
    return e * (1.0 / jnp.sum(e, 0, keepdims=True))


def attend_body(qkv, before, after, log_c, out, pairs):
    for s in range(qkv.shape[0]):
        gather_pairs(qkv, before, after, pairs, s)
        for h in range(HEADS):
            lanes = slice(h * HEAD_DIM, (h + 1) * HEAD_DIM)
            keys = pairs[:, lanes]
            values = pairs[:, D + h * HEAD_DIM : D + (h + 1) * HEAD_DIM]
            probs = attention_weights(keys, qkv[s, :, lanes], log_c)
            out_t = dot_tn(values, probs.astype(BF))
            out[s, :, lanes] = out_t.T.astype(BF)


def attend(qkv, before, after, log_c):
    samples, nodes = qkv.shape[:2]
    return kernel_call(
        attend_body,
        shape((samples, nodes, D), BF),
        [pltpu.VMEM((log_c.shape[0], 2 * D), BF)],
        nbytes=8 << 20,
        flops=2 << 30,
    )(qkv, before, after, log_c)


class Layout:
    def __init__(self, shard, devices, fast):
        self.devices = devices
        self.starts, self.win = window_plan(shard, devices)
        self.rows = 4 * self.win
        self.begins = [(LEAD * D + d * shard) // 1024 * 8 for d in range(devices)]
        self.ends = [-(-(LEAD * D + (d + 1) * shard) // 1024) * 8 for d in range(devices)]
        self.small = 4 * (ROWS_ALL - ROW_DEC)
        first = (("out", ROW_OUT, 4 * D), ("up", ROW_UP, 16 * D), ("down", ROW_DOWN, 4 * FF))
        second = (("enc", ROW_ENC, 4 * C_IN), ("qkv", ROW_QKV, 12 * D), ("small", ROW_DEC, self.small))
        self.fast = fast
        if fast:
            self.apart = 4 * (ROW_OUT - self.starts[8])
            self.sizes = (12 * self.rows, 4 * self.rows + self.apart + self.small)
        else:
            self.sizes = (sum(x[2] for x in first), sum(x[2] for x in second))
        self.plans = self.make(first, 1), self.make(second, 0)

    def make(self, arrays, plane):
        plans, k, at = {}, 0, 0
        for name, row, size in arrays:
            plans[name] = []
            if not self.fast:
                plans[name].append((k, None, at, 0, size))
                k, at = k + 1, at + size
                continue
            if name == "small":
                plans[name].append((k, "both", 4 * self.rows + self.apart, 0, size))
                k += 2
                continue
            for d, (lower, upper, start) in enumerate(zip(self.begins, self.ends, self.starts)):
                low, high = max(lower, 4 * row), min(upper, 4 * (row + size // 4))
                if low >= high:
                    continue
                if d == 8 and plane == 0:
                    to = 4 * self.rows + low - 4 * start
                    plans[name].append((k, "both", to, low - 4 * row, high - low))
                    k += 2
                else:
                    place = (d // 8 - plane) * 4 * self.rows + low - 4 * start
                    plans[name].append((k, d % 8, place, low - 4 * row, high - low))
                    k += 1
        return plans, k


def window_copies(here, rows_of_slot, blocks, source, keep, send, sems, action):
    for k, near, to, at, rows in blocks:

        def copy(target, first, sem):
            getattr(
                pltpu.make_async_copy(
                    source.at[pl.ds(at, rows), :], target.at[pl.ds(first, rows), :], sems.at[sem]
                ),
                action,
            )()

        if near is None:
            copy(keep, to, k)
        elif near == "both":
            copy(keep, to, k)
            copy(send, to, k + 1)
        else:
            slot = jnp.bitwise_and(jnp.bitwise_xor(here, near), 7)
            first = pl.multiple_of(lax.shift_right_logical(slot, 1) * rows_of_slot + to, 8)
            for target, side in ((keep, 0), (send, 1)):

                @pl.when(jnp.bitwise_and(slot, 1) == side)
                def _():
                    copy(target, first, k)


def sum_flat(first, second, layout):
    flat = jnp.concatenate(
        [
            jnp.zeros((4 * LEAD, 128), F32),
            second[: 4 * (ROW_OUT - LEAD)],
            first,
            second[4 * (ROW_OUT - LEAD) :],
            jnp.zeros((max(0, 4 * (layout.starts[-1] + layout.win - ROWS_ALL)), 128), F32),
        ]
    )
    windows = jnp.concatenate([flat[4 * s : 4 * s + layout.rows] for s in layout.starts])
    return lax.psum_scatter(windows, AXES, scatter_dimension=0, tiled=True)


def low(x):
    return x.astype(BF)


def packed(blocks, extra):
    return low(jnp.concatenate([blocks.reshape(-1, 128), extra]))


def add_packed(flat, blocks, extra):
    flat = flat.astype(F32)
    count = flat.shape[0] - extra.shape[0]
    return blocks + flat[:count].reshape(blocks.shape), extra + flat[count:]


def across_planes(x, allowed, k):
    pairs = [(d, d ^ (8 * k)) for d in range(32) if allowed((d ^ (8 * k)) // 8, d % 8)]
    return lax.ppermute(x, AXES, pairs)


def sum_rest(early, early_got, second, layout, me):
    rows = layout.rows
    half = rows // 2
    near, mine = me % 8, me // 8

    late = second[0] + permute(second[1], 1)
    early_a = early[:, :, 0, :half] + early_got[0].astype(F32)
    early_b = early[:, 0, :, half:] + early_got[1].astype(F32)
    early_a = early_a[:, 0] + permute(low(early_a[:, 1]), 4).astype(F32)
    early_b = early_b[:, 0] + permute(low(early_b[:, 1]), 2).astype(F32)
    planes = jnp.concatenate([early_a, early_b], axis=1)

    def plane(k):
        return lax.dynamic_index_in_dim(
            planes, jnp.maximum(jnp.bitwise_xor(mine, k) - 1, 0), 0, False
        )

    upper = plane(0)
    for k in (1, 2, 3):
        upper = upper + across_planes(low(plane(k)), lambda p, q: p > 0, k).astype(F32)

    apart = late[4 * rows :]
    late = late[: 4 * rows].reshape(2, 2, rows, 128)
    cut = apart.shape[0] // 2
    late_a, apart_a = add_packed(
        permute(packed(late[:, 1, :half], apart[:cut]), 2), late[:, 0, :half], apart[:cut]
    )
    late_b, apart_b = add_packed(
        permute(packed(late[1, :, half:], apart[cut:]), 4), late[0, :, half:], apart[cut:]
    )
    late_a, apart_a = add_packed(permute(packed(late_a[1], apart_a), 4), late_a[0], apart_a)
    late_b, apart_b = add_packed(permute(packed(late_b[1], apart_b), 2), late_b[0], apart_b)
    apart = jnp.concatenate([apart_a, apart_b])
    lead, small = layout.apart, 4 * (ROW_DEC - layout.starts[31])
    one = jnp.concatenate([apart[:lead], jnp.zeros((rows - lead, 128), F32)])
    three = jnp.concatenate([jnp.zeros((small, 128), F32), apart[lead : lead + rows - small]])
    parts = jnp.stack([jnp.concatenate([late_a, late_b]), one, one, three])

    def part(k):
        return lax.dynamic_index_in_dim(parts, jnp.bitwise_xor(mine, k), 0, False)

    lower = part(0)
    for k in (1, 2, 3):
        got = across_planes(
            low(part(k)), lambda p, q: p == 0 or (p, q) == (1, 0) or (p, q) == (3, 7), k
        )
        lower = lower + got.astype(F32)
    row = lax.broadcasted_iota(jnp.int32, (rows, 1), 0)
    take = (mine == 0) | ((me == 8) & (row < lead)) | ((me == 31) & (row >= small))
    return jnp.where(take, lower, upper)


def sum_everywhere(x, fast):
    if not fast:
        return lax.psum(x, AXES)
    for k in range(5):
        x = x + permute(x, 1 << k)
    return x


def mlp_body(
    layout,
    me, h0, attended, w_out, w_dec, gains, weight, levels, scale, w_up_hbm, w_down_hbm, dec_mt_hbm, targets_hbm,
    dh1, d_dec, d_gains, loss, keep, send,
    h1, n2, upper, act, h2, n3, pred, d_pred, dm, du, d_y, total_out, d_out, d_up, d_down, w_up, w_down, dec_mt, targets_t, sems, in_sems,
):
    samples, nodes, _ = h0.shape
    here = me[0]
    loads = [
        pltpu.make_async_copy(source, target, in_sems.at[k])
        for k, (source, target) in enumerate(
            ((w_up_hbm, w_up), (w_down_hbm, w_down), (dec_mt_hbm, dec_mt), (targets_hbm, targets_t))
        )
    ]
    for load in loads:
        load.start()
    pixels = dec_mt.shape[1]
    tile = 512
    tiles = nodes // tile
    for s in range(samples):

        @pl.loop(0, tiles, unroll=True)
        def _(i):
            rows = pl.ds(pl.multiple_of(i * tile, tile), tile)
            flat = pl.ds(pl.multiple_of(s * nodes + i * tile, tile), tile)
            mid = h0[s, rows, :] + dot(attended[s, rows, :], w_out[...])
            h1[flat, :] = mid
            hat, _ = norm(mid)
            in_two = (hat * gains[1:2, :]).astype(BF)
            n2[flat, :] = in_two
            if s == 0:
                loads[0].wait()
                loads[1].wait()
            end = mid
            for c in range(4):
                cols = slice(c * D, (c + 1) * D)
                u = dot(in_two, w_up[:, cols])
                sig = sigmoid(u)
                upper[flat, cols] = slope(u, sig)
                a = (u * sig).astype(BF)
                act[flat, cols] = a
                end = end + dot(a, w_down[cols, :])
            h2[flat, :] = end
            hat, _ = norm(end)
            in_three = (hat * gains[2:3, :]).astype(BF)
            n3[flat, :] = in_three
            y_t = dot(in_three, w_dec[...]).T
            high, low = split(y_t[0:CP, :])
            pred[s * CP : (s + 1) * CP, rows] = high
            pred[(samples + s) * CP : (samples + s + 1) * CP, rows] = low

    loads[2].wait()
    loads[3].wait()
    d_pred[...] = jnp.zeros(d_pred.shape, F32)
    loss[...] = jnp.zeros(loss.shape, F32)

    @pl.loop(0, pixels // 512)
    def _(i):
        part = pl.ds(pl.multiple_of(i * 512, 512), 512)
        counts = dec_mt[:, part]
        y_all = dot(pred[...], counts)
        highs, lows = [], []
        for s in range(samples):
            y = y_all[s * CP : (s + 1) * CP] + y_all[(samples + s) * CP : (samples + s + 1) * CP]
            misfit = y * (1.0 / 3.0) - targets_t[s, :, part]
            g = weight[s : s + 1, part] * levels[...] * misfit
            loss[...] += jnp.sum(g * misfit, axis=0, keepdims=True)
            high, low = split(g * scale[0:1, 0:1])
            highs.append(high)
            lows.append(low)
        d_pred[...] += dot_nt(jnp.concatenate(highs + lows, axis=0), counts)

    total_out[...] = jnp.zeros(total_out.shape, F32)
    d_dec[...] = jnp.zeros(d_dec.shape, F32)
    d_gains[...] = jnp.zeros(d_gains.shape, F32)
    for s in range(samples):
        total = d_pred[s * CP : (s + 1) * CP] + d_pred[(samples + s) * CP : (samples + s + 1) * CP]
        padded = jnp.concatenate([total, jnp.zeros((128 - CP, nodes), F32)], axis=0)
        d_y[...] = padded.T.astype(BF)

        @pl.loop(0, tiles, unroll=True)
        def _(i):
            rows = pl.ds(pl.multiple_of(i * tile, tile), tile)
            flat = pl.ds(pl.multiple_of(s * nodes + i * tile, tile), tile)
            d_part = d_y[rows, :]
            d_dec[...] += dot_tn(n3[flat, :], d_part)
            grad = dot_nt(d_part, w_dec[...])
            hat, r = norm(h2[flat, :])
            d_gains[2:3, :] += jnp.sum(grad * hat, axis=0, keepdims=True)
            d_end = norm_back(grad, gains[2:3, :], hat, r)
            d_low = d_end.astype(BF)
            dm[flat, :] = d_low
            d_in = jnp.zeros((tile, D), F32)
            for c in range(4):
                cols = slice(c * D, (c + 1) * D)
                d_act = dot_nt(d_low, w_down[cols, :])
                d_u = (d_act * upper[flat, cols]).astype(BF)
                du[flat, cols] = d_u
                d_in = d_in + dot_nt(d_u, w_up[:, cols])
            hat, r = norm(h1[flat, :])
            d_gains[1:2, :] += jnp.sum(d_in * hat, axis=0, keepdims=True)
            d_mid = d_end + norm_back(d_in, gains[1:2, :], hat, r)
            dh1[s, rows, :] = d_mid
            total_out[...] += dot_tn(attended[s, rows, :], d_mid.astype(BF))

    def copies(name, source, action):
        window_copies(
            here, layout.rows, layout.plans[0][0][name], source, keep, send, sems, action
        )

    for c in range(4):
        cols = slice(c * D, (c + 1) * D)
        put_flat(d_down, dot_tn(act[:, cols], dm[...]), 4 * c * D, 4)
    copies("down", d_down, "start")
    put_flat(d_out, total_out[...], 0, 4)
    copies("out", d_out, "start")
    for c in range(4):
        cols = slice(c * D, (c + 1) * D)
        put_flat(d_up, dot_tn(n2[...], du[:, cols]), 4 * c, 16)
    copies("up", d_up, "start")
    copies("down", d_down, "wait")
    copies("out", d_out, "wait")
    copies("up", d_up, "wait")


def mlp(me, h0, attended, w_out, w_up, w_down, w_dec, gains, dec_mt, targets_t, weight, levels, scale, layout):
    samples, nodes, _ = h0.shape
    rows = samples * nodes
    count = layout.plans[0][1]
    sent = layout.sizes[0] if layout.fast else 8
    vmem = pl.BlockSpec(memory_space=pltpu.VMEM)
    hbm = pl.BlockSpec(memory_space=pl.ANY)
    return pl.pallas_call(
        functools.partial(mlp_body, layout),
        out_shape=[
            shape((samples, nodes, D)),
            shape((D, 128)),
            shape((8, D)),
            shape((1, 512)),
            shape((layout.sizes[0], 128)),
            shape((sent, 128)),
        ],
        in_specs=[pl.BlockSpec(memory_space=pltpu.SMEM)] + [vmem] * 8 + [hbm] * 4,
        out_specs=[vmem] * 4 + [hbm] * 2,
        scratch_shapes=[
            pltpu.VMEM((rows, D), F32),
            pltpu.VMEM((rows, D), BF),
            pltpu.VMEM((rows, FF), F32),
            pltpu.VMEM((rows, FF), BF),
            pltpu.VMEM((rows, D), F32),
            pltpu.VMEM((rows, D), BF),
            pltpu.VMEM((2 * samples * CP, nodes), BF),
            pltpu.VMEM((2 * samples * CP, nodes), F32),
            pltpu.VMEM((rows, D), BF),
            pltpu.VMEM((rows, FF), BF),
            pltpu.VMEM((nodes, 128), BF),
            pltpu.VMEM((D, D), F32),
            pltpu.VMEM((4 * D, 128), F32),
            pltpu.VMEM((16 * D, 128), F32),
            pltpu.VMEM((4 * FF, 128), F32),
            pltpu.VMEM(w_up.shape, BF),
            pltpu.VMEM(w_down.shape, BF),
            pltpu.VMEM(dec_mt.shape, BF),
            pltpu.VMEM(targets_t.shape, F32),
            pltpu.SemaphoreType.DMA((count,)),
            pltpu.SemaphoreType.DMA((4,)),
        ],
        compiler_params=pltpu.CompilerParams(vmem_limit_bytes=60 << 20),
        cost_estimate=pl.CostEstimate(flops=16 << 30, bytes_accessed=24 << 20, transcendentals=0),
    )(me, h0, attended, w_out, w_dec, gains, weight, levels, scale, w_up, w_down, dec_mt, targets_t)


def attend_back_body(
    qkv, before, after, log_c, dh1, w_out,
    d_qkv, d_rims, d_before, d_after,
    pairs, do_both,
):
    samples, nodes, _ = dh1.shape
    halo = before.shape[1]
    for s in range(samples):
        gather_pairs(qkv, before, after, pairs, s)
        for i in range(nodes // 256):
            rows = slice(i * 256, (i + 1) * 256)
            da = dh1[s, rows, :].astype(BF)
            high, low = split(dot_nt(da, w_out[...]))
            for h in range(HEADS):
                lanes = slice(h * HEAD_DIM, (h + 1) * HEAD_DIM)
                do_both[rows, 2 * h * HEAD_DIM : (2 * h + 1) * HEAD_DIM] = high[:, lanes]
                do_both[rows, (2 * h + 1) * HEAD_DIM : (2 * h + 2) * HEAD_DIM] = low[:, lanes]
        for h in range(HEADS):
            lanes = slice(h * HEAD_DIM, (h + 1) * HEAD_DIM)
            vlanes = slice(D + h * HEAD_DIM, D + (h + 1) * HEAD_DIM)
            query = qkv[s, :, lanes]
            keys = pairs[:, lanes]
            values = pairs[:, vlanes]
            do = do_both[:, 2 * h * HEAD_DIM : (2 * h + 2) * HEAD_DIM]
            probs = attention_weights(keys, query, log_c)
            d_probs = dot_nt(jnp.concatenate([values, values], axis=1), do)
            centre = jnp.sum(probs * d_probs, 0, keepdims=True)
            high, low = split(probs * (d_probs - centre))
            dv2 = dot(probs.astype(BF), do)
            dv = dv2[:, :HEAD_DIM] + dv2[:, HEAD_DIM:]
            dk = (dot(high, query) + dot(low, query)) * SCALE
            dq_t = (dot_tn(keys, high) + dot_tn(keys, low)) * SCALE
            d_qkv[s, :, lanes] = dq_t.T.astype(BF)
            klanes = slice(D + h * HEAD_DIM, D + (h + 1) * HEAD_DIM)
            wide_lanes = slice(2 * D + h * HEAD_DIM, 2 * D + (h + 1) * HEAD_DIM)
            d_qkv[s, :, klanes] = dk[halo : halo + nodes].astype(BF)
            d_qkv[s, :, wide_lanes] = dv[halo : halo + nodes].astype(BF)
            for rim, first in ((0, halo), (1, nodes)):
                d_rims[s, rim, :, lanes] = dk[first : first + halo]
                d_rims[s, rim, :, vlanes] = dv[first : first + halo]
            d_before[s, :, lanes] = dk[:halo].astype(BF)
            d_before[s, :, vlanes] = dv[:halo].astype(BF)
            d_after[s, :, lanes] = dk[halo + nodes :].astype(BF)
            d_after[s, :, vlanes] = dv[halo + nodes :].astype(BF)


def attend_back(qkv, before, after, log_c, dh1, w_out):
    samples, nodes, _ = dh1.shape
    halo = before.shape[1]
    return kernel_call(
        attend_back_body,
        [
            shape((samples, nodes, 3 * D), BF),
            shape((samples, 2, halo, 2 * D)),
            shape((samples, halo, 2 * D), BF),
            shape((samples, halo, 2 * D), BF),
        ],
        [pltpu.VMEM((log_c.shape[0], 2 * D), BF), pltpu.VMEM((nodes, 2 * D), BF)],
        nbytes=20 << 20,
        flops=8 << 30,
    )(qkv, before, after, log_c, dh1, w_out)


def encode_back_body(
    layout,
    me, grid, w_enc, w_qkv, gains, enc_mt, h0, dh1, d_in, d_rims, from_lower, from_upper,
    d_small,
    keep, send,
    dqkv, n1, both, total_enc, d_gain, d_enc, d_qkv, small, sems,
):
    samples, nodes, _ = h0.shape
    here = me[0]

    def copies(name, source, action):
        window_copies(
            here, layout.rows, layout.plans[1][0][name], source, keep, send, sems, action
        )

    small[...] = d_small[...]
    pixels = grid.shape[2]
    halo = from_lower.shape[1]
    d_gain[...] = jnp.zeros(d_gain.shape, F32)
    total_enc[...] = jnp.zeros(total_enc.shape, F32)
    for s in range(samples):
        base = s * nodes
        dqkv[base : base + nodes, :] = d_in[s]
        low_rim = d_rims[s, 0] + from_lower[s].astype(F32)
        dqkv[base : base + halo, D:] = low_rim.astype(BF)
        high_rim = d_rims[s, 1] + from_upper[s].astype(F32)
        dqkv[base + nodes - halo : base + nodes, D:] = high_rim.astype(BF)
        for i in range(nodes // 256):
            rows = slice(i * 256, (i + 1) * 256)
            flat = slice(base + i * 256, base + (i + 1) * 256)
            hat, r = norm(h0[s, rows, :])
            n1[flat, :] = (hat * gains[0:1, :]).astype(BF)
            grad = dot_nt(dqkv[flat, :], w_qkv[...])
            d_gain[0:1, :] += jnp.sum(grad * hat, axis=0, keepdims=True)
            d_start = dh1[s, rows, :] + norm_back(grad, gains[0:1, :], hat, r)
            high, low = split(d_start * 0.25)
            both[rows, 0:D] = high
            both[rows, D:] = low

        @pl.loop(0, pixels // 512, unroll=True)
        def _(i):
            rows = pl.ds(pl.multiple_of(i * 512, 512), 512)
            x_t = grid[s, :, rows]
            pre = dot_tn(x_t, w_enc[...])
            spread2 = dot(enc_mt[rows, :], both[...])
            spread = spread2[:, 0:D] + spread2[:, D:]
            d_pre = (spread * slope(pre, sigmoid(pre))).astype(BF)
            total_enc[...] += dot(x_t, d_pre)

    for c in range(3):
        put_flat(d_qkv, dot_tn(n1[...], dqkv[:, c * D : (c + 1) * D]), 4 * c, 12)
    copies("qkv", d_qkv, "start")
    put_flat(d_enc, total_enc[...], 0, 4)
    for lane in range(D // 128):
        row = 4 * C_OUT + lane
        small[row : row + 1, :] = d_gain[0:1, lane * 128 : lane * 128 + 128]
    for action in ("start", "wait"):
        copies("enc", d_enc, action)
        copies("small", small, action)
        if action == "wait":
            copies("qkv", d_qkv, action)


def encode_back(me, grid, w_enc, w_qkv, gains, enc_mt, h0, dh1, d_in, d_rims, from_lower, from_upper,
                d_small, layout):
    samples, nodes, _ = h0.shape
    rows = samples * nodes
    vmem = pl.BlockSpec(memory_space=pltpu.VMEM)
    hbm = pl.BlockSpec(memory_space=pl.ANY)
    return pl.pallas_call(
        functools.partial(encode_back_body, layout),
        out_shape=[shape((layout.sizes[1], 128)), shape((layout.sizes[1] if layout.fast else 8, 128))],
        in_specs=[pl.BlockSpec(memory_space=pltpu.SMEM)] + [vmem] * 12,
        out_specs=[hbm, hbm],
        scratch_shapes=[
            pltpu.VMEM((rows, 3 * D), BF),
            pltpu.VMEM((rows, D), BF),
            pltpu.VMEM((nodes, 2 * D), BF),
            pltpu.VMEM((C_IN, D), F32),
            pltpu.VMEM((8, D), F32),
            pltpu.VMEM((4 * C_IN, 128), F32),
            pltpu.VMEM((12 * D, 128), F32),
            pltpu.VMEM(d_small.shape, F32),
            pltpu.SemaphoreType.DMA((layout.plans[1][1],)),
        ],
        compiler_params=pltpu.CompilerParams(vmem_limit_bytes=58 << 20),
        cost_estimate=pl.CostEstimate(flops=12 << 30, bytes_accessed=24 << 20, transcendentals=0),
    )(me, grid, w_enc, w_qkv, gains, enc_mt, h0, dh1, d_in, d_rims, from_lower, from_upper, d_small)


def ring(axis, distance):
    count = lax.axis_size(axis)
    return [(i, (i + distance) % count) for i in range(count)]


def window_plan(shard, count):
    starts = [(LEAD * D + d * shard) // (16 * D) * 16 for d in range(count)]
    ends = [-(-(LEAD * D + (d + 1) * shard) // D) for d in range(count)]
    rows = max(-(-(e - s + 1) // 16) * 16 for s, e in zip(starts, ends))
    return starts, rows


def per_device(
    grid, targets, area, sigma_weight, level_weight, valid, enc_index, dec_index, neighbours,
    params, first_moment, second_moment, average,
):
    shard = params.shape[0]
    devices = lax.axis_size(AXES)
    me = lax.axis_index(AXES)
    nodes = neighbours.shape[0]
    halo = nodes // 16
    fast = (lax.axis_size("patch"), lax.axis_size("dp")) == (8, 4)
    layout = Layout(shard, devices, fast)
    starts, win = layout.starts, layout.win
    begin = LEAD * D + me * shard
    shift = begin - begin // (16 * D) * (16 * D)
    place = me.astype(jnp.int32).reshape(1)

    count = jnp.sum(valid)
    digits = jnp.stack([count // 128, count % 128]).astype(BF)
    payload = lax.dynamic_update_slice(jnp.zeros((win * D,), BF), params.astype(BF), (shift,))
    payload = lax.dynamic_update_slice(payload, digits, ((win - 1) * D,)).reshape(win, D)
    weight = valid.astype(F32) * area[None, :] * sigma_weight[:, None]
    levels = jnp.pad(level_weight, (0, CP - C_OUT)).reshape(CP, 1)
    pixels = dec_index.shape[0]
    first_work = lambda: count_encoder(enc_index, pixels)
    positions = me * shard + lax.iota(jnp.int32, shard)
    bounds = segment_bounds() + [(-1, -1)]
    lower = jnp.array([x for x, _ in bounds], jnp.int32)[:, None]
    upper = jnp.array([x for _, x in bounds], jnp.int32)[:, None]
    member = ((positions >= lower) & (positions < upper)).astype(F32)
    second_work = lambda: (count_rest(dec_index, neighbours, targets), weight, levels, member)
    if fast:
        pieces, plan, first_done, second_done = gather_windows(payload, first_work, second_work)
        place_of = place_by_xor
    else:
        everything = lax.all_gather(payload, AXES, axis=0, tiled=False)
        pieces = [everything.reshape(devices * win, D)]
        plan = [(0, d * win, d, 0, win) for d in range(devices)]
        place_of = lambda here, d: d
        first_done, second_done = first_work(), second_work()
    enc_m, enc_mt = first_done
    (dec_mt, log_c, targets_t), weight, levels, member = second_done
    grid = jnp.swapaxes(grid, 1, 2)

    w_enc, w_qkv, head = unpack(
        place, pieces, plan, ("enc", "qkv", "gain"), place_of, devices, win, starts
    )
    h0, qkv = encode(grid, w_enc, enc_m, w_qkv, head)
    before = lax.ppermute(qkv[:, nodes - halo :, D:], "patch", ring("patch", 1))
    after = lax.ppermute(qkv[:, :halo, D:], "patch", ring("patch", -1))
    w_out, w_up, w_down, tail, counted = unpack(
        place, pieces, plan, ("out", "up", "down", "tail", "count"), place_of, devices, win, starts
    )
    w_dec = jnp.pad(tail[:C_OUT].reshape(D, C_OUT), ((0, 0), (0, 128 - C_OUT)))
    gains = jnp.pad(tail[C_OUT : C_OUT + 3].astype(F32), ((0, 5), (0, 0)))
    count_total = counted[0, 0]
    attended = attend(qkv, before, after, log_c)
    scale = 2.0 / counted * (1.0 / 3.0)
    dh1, d_dec, d_gains, loss_rows, keep, send = mlp(
        place, h0, attended, w_out, w_up, w_down, w_dec, gains, dec_mt, targets_t, weight, levels,
        scale, layout,
    )
    if fast:
        summed = keep + permute(send, 1)
    d_qkv, d_rims, d_before, d_after = attend_back(qkv, before, after, log_c, dh1, w_out)
    from_upper = lax.ppermute(d_before, "patch", ring("patch", -1))
    from_lower = lax.ppermute(d_after, "patch", ring("patch", 1))
    d_small = jnp.concatenate(
        [
            d_dec[:, :C_OUT].reshape(4 * C_OUT, 128),
            jnp.zeros((4, 128), F32),
            d_gains[1:3].reshape(8, 128),
            jnp.zeros((4 * (ROWS_ALL - ROW_END), 128), F32),
        ]
    )
    if fast:
        summed, d_qkv, from_upper, from_lower, d_small = lax.optimization_barrier(
            (summed, d_qkv, from_upper, from_lower, d_small)
        )
        half = layout.rows // 2
        early = summed.reshape(3, 2, 2, layout.rows, 128)
        got = permute(low(early[:, :, 1, :half]), 2), permute(low(early[:, 1, :, half:]), 4)
    second = encode_back(
        place, grid, w_enc, w_qkv, gains, enc_mt, h0, dh1, d_qkv, d_rims, from_lower, from_upper,
        d_small, layout,
    )
    if fast:
        second, got = lax.optimization_barrier((second, got))
        grad_window = sum_rest(early, got, second, layout, me)
    else:
        grad_window = sum_flat(keep, second[0], layout)
    grad = lax.dynamic_slice(grad_window.reshape(-1), (shift,), (shard,))

    new_first = BETA_ONE * first_moment + (1.0 - BETA_ONE) * grad
    new_second = BETA_TWO * second_moment + (1.0 - BETA_TWO) * grad * grad
    update = (
        new_first
        / (1.0 - BETA_ONE**STEP)
        / (jnp.sqrt(new_second / (1.0 - BETA_TWO**STEP)) + LAMB_EPS)
        + DECAY * params
    )
    both = jnp.stack([params * params, update * update])
    sums = jnp.sum(member[None] * both[:, None, :], axis=2)
    loss_at = (jnp.arange(2)[:, None] == 0) & (jnp.arange(8)[None, :] == 7)
    sums = jnp.where(loss_at, jnp.sum(loss_rows), sums)
    totals = sum_everywhere(sums, fast)
    norms = jnp.sqrt(totals[:, :7])
    step_ratio = jnp.sum(member[:7] * (norms[0] / norms[1])[:, None], axis=0)
    new_params = params - RATE * step_ratio * update
    new_average = EMA_KEEP * average + (1.0 - EMA_KEEP) * new_params
    return (
        jnp.stack([totals[0, 7], count_total]),
        norms,
        new_params,
        new_first,
        new_second,
        new_average,
    )


def solution(mesh):
    flat = P(AXES)
    in_specs = (
        P("dp", "patch", None),
        P("dp", "patch", None),
        P("patch"),
        P("dp"),
        P(),
        P("dp", "patch"),
        P("patch", None),
        P("patch", None),
        P("patch", None),
        flat,
        flat,
        flat,
        flat,
    )
    out_specs = (P(), P(), flat, flat, flat, flat)
    return jax.shard_map(
        per_device, mesh=mesh, in_specs=in_specs, out_specs=out_specs, check_vma=False
    )
```

profile of v0, /device:TPU:0, one launch (start us, length us, event | category | flops | bytes accessed | tf_op | source)
XLA Modules:
  0.0 293.5 jit_solution(857736853691508897)
XLA Ops:
  0.7 1.4 reduce_sum.36
  5.8 2.0 dynamic_update_slice.6
  8.3 5.1 %collective-permute-start.3 = (bf16[224,512]{1,0:T(8,128)(2,1)S(1)}, bf16[224,512]{1,0:T(8,128)(2,1)S(1)}, u32[]{:S(2)}, u32[]{:S(2)}) collective-permute-start(bf16[224,512]{1,0:T(8,128)(2,1)S(1)} %reshape.103.refs_1_), channel_id=1, source_target_pairs={{0,24},{1,25},{2,26},{3,27},{4,28},{5,29},{6,30},{7,31},{8,16},{9,... | collective-permute-start | bytes 688136 | tf_op jit(solution)/shard_map/ppermute | solution.py:332
  14.0 1.6 collective-permute-start.4
  15.6 1.5 collective-permute-start.5
  18.8 7.9 %shard_map.190 = (bf16[512,2048]{1,0:T(8,128)(2,1)}, bf16[2048,512]{1,0:T(8,128)(2,1)}) custom-call(s32[512,4]{1,0:T(8,128)} %copy.31.enc, s32[4,512]{1,0:T(4,128)} %bitcast.117), custom_call_target="tpu_custom_call" | custom-call | flops 536870912 | bytes 5242880 | tf_op jit(solution)/shard_map/pallas_call | solution.py:174
  26.7 6.2 %collective-permute-done.2 = bf16[224,512]{1,0:T(8,128)(2,1)S(1)} collective-permute-done((bf16[224,512]{1,0:T(8,128)(2,1)S(1)}, bf16[224,512]{1,0:T(8,128)(2,1)S(1)}, u32[]{:S(2)}, u32[]{:S(2)}) %collective-permute-start.2) | collective-permute-done | bytes 229408 | tf_op jit(solution)/shard_map/ppermute | solution.py:332
  33.8 1.6 collective-permute-start.9
  35.4 1.5 collective-permute-start.10
  38.1 3.6 %copy.32.targets = f32[2,2048,84]{2,1,0:T(8,128)} copy(f32[2,2048,84]{1,0,2:T(2,128)} %param.16) | data formatting | bytes 2752512 | tf_op args[1]
  41.8 8.7 %shard_map.191 = (bf16[512,2048]{1,0:T(8,128)(2,1)}, f32[576,512]{1,0:T(8,128)}, f32[2,96,2048]{2,1,0:T(8,128)}) custom-call(s32[3,2048]{1,0:T(4,128)} %bitcast.115, s32[16,512]{1,0:T(8,128)} %bitcast.116, f32[2,2048,84]{2,1,0:T(8,128)} %copy.32.targets), custom_call_target="tpu_custom_call" | custom-call | flops 536870912 | bytes 8388608 | tf_op jit(solution)/shard_map/pallas_call | solution.py:185
  54.4 1.5 collective-permute-start.15
  57.1 9.0 %collective-permute-done.13.refs_13_ = bf16[448,512]{1,0:T(8,128)(2,1)} collective-permute-done((bf16[448,512]{1,0:T(8,128)(2,1)S(1)}, bf16[448,512]{1,0:T(8,128)(2,1)}, u32[]{:S(2)}, u32[]{:S(2)}) %collective-permute-start.13) | collective-permute-done | bytes 458784 | tf_op jit(solution)/shard_map/ppermute | solution.py:332
  66.7 1.4 copy.33.levels
  69.0 5.3 %shard_map.192 = (bf16[264,512]{1,0:T(8,128)(2,1)}, bf16[512,1536]{1,0:T(8,128)(2,1)}, f32[8,512]{1,0:T(8,128)}) custom-call(s32[1]{0:T(128)} %bitcast.refs_0_.me, bf16[224,512]{1,0:T(8,128)(2,1)} %copy-done.6, bf16[224,512]{1,0:T(8,128)(2,1)} %collective-permute-done.refs_2_, bf16[224,512]{1,0:T(8,128)(2,1)} %copy-done.10, bf16[224,512]{1,0:T(8,128)(2,1)} %copy-done.15, ...), custom_call_target="tpu_custom_call" | custom-call | bytes 14680064 | tf_op jit(solution)/shard_map/pallas_call | solution.py:313
  74.3 13.4 %shard_map.193 = (f32[2,512,512]{2,1,0:T(8,128)}, bf16[2,512,1536]{2,1,0:T(8,128)(2,1)}) custom-call(bf16[2,264,2048]{2,1,0:T(8,128)(2,1)} %bitcast.118, bf16[264,512]{1,0:T(8,128)(2,1)} %get-tuple-element.65.w_enc, bf16[512,2048]{1,0:T(8,128)(2,1)} %get-tuple-element.66.enc_m, bf16[512,1536]{1,0:T(8,128)(2,1)} %get-tuple-element.67.w_qkv, ...), custom_call_target="tpu_custom_call" | custom-call | flops 8589934592 | bytes 12582912 | tf_op jit(solution)/shard_map/pallas_call | solution.py:406
  87.7 1.7 fusion.43
  89.9 4.4 %collective-permute-start.18 = (bf16[2,32,1024]{2,1,0:T(8,128)(2,1)}, bf16[2,32,1024]{2,1,0:T(8,128)(2,1)}, u32[]{:S(2)}, u32[]{:S(2)}) collective-permute-start(bf16[2,32,1024]{2,1,0:T(8,128)(2,1)} %get-tuple-element.109), channel_id=1, source_target_pairs={{0,28},{4,0},{8,4},{12,8},{16,12},{20,16},{24,20},{28,24},{1,29},{... | collective-permute-start | bytes 393224 | tf_op jit(solution)/shard_map/ppermute | solution.py:1000
  94.4 6.8 %shard_map.195 = (bf16[512,512]{1,0:T(8,128)(2,1)}, bf16[512,2048]{1,0:T(8,128)(2,1)}, bf16[2048,512]{1,0:T(8,128)(2,1)}, bf16[96,512]{1,0:T(8,128)(2,1)}, f32[8,128]{1,0:T(8,128)}) custom-call(s32[1]{0:T(128)} %bitcast.refs_0_.me, bf16[224,512]{1,0:T(8,128)(2,1)} %copy-done.6, bf16[224,512]{1,0:T(8,128)(2,1)} %collective-permute-done.refs_2_, ...), custom_call_target="tpu_custom_call" | custom-call | bytes 14680064 | tf_op jit(solution)/shard_map/pallas_call | solution.py:313
  105.8 8.6 %shard_map.194.attended = bf16[2,512,512]{2,1,0:T(8,128)(2,1)} custom-call(bf16[2,512,1536]{2,1,0:T(8,128)(2,1)} %get-tuple-element.70.qkv, bf16[2,32,1024]{2,1,0:T(8,128)(2,1)} %collective-permute-done.17.before, bf16[2,32,1024]{2,1,0:T(8,128)(2,1)} %collective-permute-done.18.after, f32[576,512]{1,0:T(8,128)} %get-tuple-element.71.log_c), custom_call_target="tpu_custom_call" | custom-call | flops 2147483648 | bytes 8388608 | tf_op jit(solution)/shard_map/pallas_call | solution.py:442
  114.4 40.6 %shard_map.196 = (f32[2,512,512]{2,1,0:T(8,128)}, f32[512,128]{1,0:T(8,128)}, f32[8,512]{1,0:T(8,128)}, f32[1,512]{1,0:T(1,128)}, f32[10752,128]{1,0:T(8,128)}, /*index=5*/f32[10752,128]{1,0:T(8,128)}) custom-call(s32[1]{0:T(128)} %bitcast.refs_0_.me, f32[2,512,512]{2,1,0:T(8,128)} %get-tuple-element.69.h0, bf16[2,512,512]{2,1,0:T(8,128)(2,1)} %shard_map.194.attended, ...), custom_call_target="tpu_custom_call" | custom-call | flops 17179869184 | bytes 25165824 | tf_op jit(solution)/shard_map/pallas_call | solution.py:747
  155.3 18.1 %shard_map.197 = (bf16[2,512,1536]{2,1,0:T(8,128)(2,1)}, f32[2,2,32,1024]{3,2,1,0:T(8,128)}, bf16[2,32,1024]{2,1,0:T(8,128)(2,1)}, bf16[2,32,1024]{2,1,0:T(8,128)(2,1)}) custom-call(bf16[2,512,1536]{2,1,0:T(8,128)(2,1)} %get-tuple-element.70.qkv, bf16[2,32,1024]{2,1,0:T(8,128)(2,1)} %collective-permute-done.17.before, ...), custom_call_target="tpu_custom_call" | custom-call | flops 8589934592 | bytes 20971520 | tf_op jit(solution)/shard_map/pallas_call | solution.py:836
  173.4 2.0 collective-permute-start.21
  178.1 4.7 %add.152 = f32[10752,128]{1,0:T(8,128)S(1)} add(f32[10752,128]{1,0:T(8,128)} %get-tuple-element.85, f32[10752,128]{1,0:T(8,128)} %collective-permute-done.19) | non-fusion elementwise | flops 1376256 | bytes 16515072 | tf_op jit(solution)/shard_map/add | solution.py:1014
  183.0 2.3 copy-done
  186.6 19.9 %shard_map.198 = (f32[4736,128]{1,0:T(8,128)}, f32[4736,128]{1,0:T(8,128)}) custom-call(s32[1]{0:T(128)} %bitcast.refs_0_.me, bf16[2,264,2048]{2,1,0:T(8,128)(2,1)} %bitcast.119, bf16[264,512]{1,0:T(8,128)(2,1)} %get-tuple-element.65.w_enc, bf16[512,1536]{1,0:T(8,128)(2,1)} %get-tuple-element.67.w_qkv, f32[8,512]{1,0:T(8,128)} %pad_convert_fusion.gains, ...), custom_call_target="tpu_custom_call" | custom-call | flops 12884901888 | bytes 25165824 | tf_op jit(solution)/shard_map/pallas_call | solution.py:919
  206.7 1.7 fusion.1
  208.4 2.1 collective-permute-start.32
  210.5 1.7 fusion
  213.2 1.9 add.153
  217.2 1.9 collective-permute-done.32
  219.2 3.9 %collective-permute-done.33 = bf16[3,448,128]{2,1,0:T(8,128)(2,1)S(1)} collective-permute-done((bf16[3,448,128]{2,1,0:T(8,128)(2,1)S(1)}, bf16[3,448,128]{2,1,0:T(8,128)(2,1)S(1)}, u32[]{:S(2)}, u32[]{:S(2)}) %collective-permute-start.33) | collective-permute-done | bytes 344096 | tf_op jit(solution)/shard_map/ppermute | solution.py:332
  223.2 7.2 %collective-permute-done.25 = bf16[1472,128]{1,0:T(8,128)(2,1)S(1)} collective-permute-done((bf16[1472,128]{1,0:T(8,128)(2,1)S(1)}, bf16[1472,128]{1,0:T(8,128)(2,1)S(1)}, u32[]{:S(2)}, u32[]{:S(2)}) %collective-permute-start.25) | collective-permute-done | bytes 376864 | tf_op jit(solution)/shard_map/ppermute | solution.py:332
  233.3 4.7 %collective-permute-start.36 = (bf16[896,128]{1,0:T(8,128)(2,1)S(1)}, bf16[896,128]{1,0:T(8,128)(2,1)S(1)}, u32[]{:S(2)}, u32[]{:S(2)}) collective-permute-start(bf16[896,128]{1,0:T(8,128)(2,1)S(1)} %get-tuple-element.124), channel_id=1, source_target_pairs={{0,24},{1,25},{2,26},{3,27},{4,28},{5,29},{6,30},{7,31},{8,16},{9,... | collective-permute-start | bytes 688136 | tf_op jit(solution)/shard_map/ppermute | solution.py:552
  238.0 2.0 collective-permute-start.35
  240.0 2.5 collective-permute-start.34
  245.8 1.3 collective-permute-start.31
  247.1 1.3 collective-permute-start.30
  248.4 4.3 %collective-permute-start.29 = (bf16[896,128]{1,0:T(8,128)(2,1)}, bf16[896,128]{1,0:T(8,128)(2,1)}, u32[]{:S(2)}, u32[]{:S(2)}) collective-permute-start(bf16[896,128]{1,0:T(8,128)(2,1)} %get-tuple-element.117), channel_id=1, source_target_pairs={{0,8},{8,0},{9,1},{10,2},{11,3},{12,4},{13,5},{14,6},{15,7},{23,31}} | collective-permute-start | bytes 688136 | tf_op jit(solution)/shard_map/ppermute | solution.py:552
  254.3 1.4 reduce_sum.37
  255.9 8.7 %collective-permute-done.30 = bf16[896,128]{1,0:T(8,128)(2,1)} collective-permute-done((bf16[896,128]{1,0:T(8,128)(2,1)}, bf16[896,128]{1,0:T(8,128)(2,1)}, u32[]{:S(2)}, u32[]{:S(2)}) %collective-permute-start.30) | collective-permute-done | bytes 229408 | tf_op jit(solution)/shard_map/ppermute | solution.py:552
  265.5 1.8 fusion.12
  269.2 1.4 multiply_reduce_fusion
  274.4 2.5 collective-permute-done.38
  277.4 3.0 %collective-permute-done.39 = f32[2,8]{1,0:T(2,128)S(1)} collective-permute-done((f32[2,8]{1,0:T(2,128)S(1)}, f32[2,8]{1,0:T(2,128)S(1)}, u32[]{:S(2)}, u32[]{:S(2)}) %collective-permute-start.39) | collective-permute-done | bytes 96 | tf_op jit(solution)/shard_map/ppermute | solution.py:332
  280.4 3.6 %collective-permute-done.40 = f32[2,8]{1,0:T(2,128)S(1)} collective-permute-done((f32[2,8]{1,0:T(2,128)S(1)}, f32[2,8]{1,0:T(2,128)S(1)}, u32[]{:S(2)}, u32[]{:S(2)}) %collective-permute-start.40) | collective-permute-done | bytes 96 | tf_op jit(solution)/shard_map/ppermute | solution.py:332
  285.2 3.3 %collective-permute-done.41 = f32[2,8]{1,0:T(2,128)S(1)} collective-permute-done((f32[2,8]{1,0:T(2,128)S(1)}, f32[2,8]{1,0:T(2,128)S(1)}, u32[]{:S(2)}, u32[]{:S(2)}) %collective-permute-start.41) | collective-permute-done | bytes 96 | tf_op jit(solution)/shard_map/ppermute | solution.py:332
  290.2 1.9 pad_maximum_fusion.11
  (198 shorter events, 44.5 us)
Async XLA Ops:
  0.6 17.3 %copy-start.20 = (s32[512,4]{0,1:T(4,128)S(1)}, s32[512,4]{0,1:T(4,128)}, u32[]{:S(2)}) copy-start(s32[512,4]{0,1:T(4,128)} %param.21) | copy-start | bytes 24580
  8.2 29.8 %copy-start.6 = (bf16[224,512]{1,0:T(8,128)(2,1)}, bf16[224,512]{1,0:T(8,128)(2,1)S(1)}, u32[]{:S(2)}) copy-start(bf16[224,512]{1,0:T(8,128)(2,1)S(1)} %reshape.103.refs_1_) | copy-start | bytes 688132
  8.3 18.4 %collective-permute-start.3 = (bf16[224,512]{1,0:T(8,128)(2,1)S(1)}, bf16[224,512]{1,0:T(8,128)(2,1)S(1)}, u32[]{:S(2)}, u32[]{:S(2)}) collective-permute-start(bf16[224,512]{1,0:T(8,128)(2,1)S(1)} %reshape.103.refs_1_), channel_id=1, source_target_pairs={{0,24},{1,25},{2,26},{3,27},{4,28},{5,29},{6,30},{7,31},{8,16},{9,... | collective-permute-start | bytes 688136 | tf_op jit(solution)/shard_map/ppermute | solution.py:332
  13.4 19.5 %collective-permute-start.2 = (bf16[224,512]{1,0:T(8,128)(2,1)S(1)}, bf16[224,512]{1,0:T(8,128)(2,1)S(1)}, u32[]{:S(2)}, u32[]{:S(2)}) collective-permute-start(bf16[224,512]{1,0:T(8,128)(2,1)S(1)} %reshape.103.refs_1_), channel_id=1, source_target_pairs={{0,16},{1,17},{2,18},{3,19},{4,20},{5,21},{6,22},{7,23},{8,24},{9,... | collective-permute-start | bytes 688136 | tf_op jit(solution)/shard_map/ppermute | solution.py:332
  13.4 19.5 %collective-permute-start.1 = (bf16[224,512]{1,0:T(8,128)(2,1)S(1)}, bf16[224,512]{1,0:T(8,128)(2,1)S(1)}, u32[]{:S(2)}, u32[]{:S(2)}) collective-permute-start(bf16[224,512]{1,0:T(8,128)(2,1)S(1)} %reshape.103.refs_1_), channel_id=1, source_target_pairs={{0,8},{1,9},{2,10},{3,11},{4,12},{5,13},{6,14},{7,15},{8,0},{9,1},... | collective-permute-start | bytes 688136 | tf_op jit(solution)/shard_map/ppermute | solution.py:332
  14.0 19.8 %collective-permute-start.4 = (bf16[224,512]{1,0:T(8,128)(2,1)S(1)}, bf16[224,512]{1,0:T(8,128)(2,1)S(1)}, u32[]{:S(2)}, u32[]{:S(2)}) collective-permute-start(bf16[224,512]{1,0:T(8,128)(2,1)S(1)} %reshape.103.refs_1_), channel_id=1, source_target_pairs={{0,2},{1,3},{2,0},{3,1},{4,6},{5,7},{6,4},{7,5},{8,10},{9,11},{10,... | collective-permute-start | bytes 688136 | tf_op jit(solution)/shard_map/ppermute | solution.py:332
  15.6 18.2 %collective-permute-start.5 = (bf16[224,512]{1,0:T(8,128)(2,1)S(1)}, bf16[224,512]{1,0:T(8,128)(2,1)S(1)}, u32[]{:S(2)}, u32[]{:S(2)}) collective-permute-start(bf16[224,512]{1,0:T(8,128)(2,1)S(1)} %reshape.103.refs_1_), channel_id=1, source_target_pairs={{0,4},{1,5},{2,6},{3,7},{4,0},{5,1},{6,2},{7,3},{8,12},{9,13},{10,... | collective-permute-start | bytes 688136 | tf_op jit(solution)/shard_map/ppermute | solution.py:332
  18.8 18.1 %copy-start.7 = (s32[103920]{0:T(1024)S(1)}, s32[103920]{0:T(1024)}, u32[]{:S(2)}) copy-start(s32[103920]{0:T(1024)} %iota_add_fusion) | copy-start | bytes 1247044
  26.7 29.1 %collective-permute-start = (bf16[224,512]{1,0:T(8,128)(2,1)S(1)}, bf16[224,512]{1,0:T(8,128)(2,1)}, u32[]{:S(2)}, u32[]{:S(2)}) collective-permute-start(bf16[224,512]{1,0:T(8,128)(2,1)S(1)} %reshape.103.refs_1_), channel_id=1, source_target_pairs={{0,1},{1,0},{2,3},{3,2},{4,5},{5,4},{6,7},{7,6},{8,9},{9,8},{10,11... | collective-permute-start | bytes 688136 | tf_op jit(solution)/shard_map/ppermute | solution.py:332
  33.8 18.5 %collective-permute-start.9 = (bf16[672,512]{1,0:T(8,128)(2,1)}, bf16[672,512]{1,0:T(8,128)(2,1)}, u32[]{:S(2)}, u32[]{:S(2)}) collective-permute-start(bf16[672,512]{1,0:T(8,128)(2,1)} %pad_maximum_fusion.2.refs_7_), channel_id=1, source_target_pairs={{0,2},{1,3},{2,0},{3,1},{4,6},{5,7},{6,4},{7,5},{8,10},{9,11},{10,... | collective-permute-start | bytes 2064392 | tf_op jit(solution)/shard_map/ppermute | solution.py:332
  35.4 16.9 %collective-permute-start.10 = (bf16[672,512]{1,0:T(8,128)(2,1)}, bf16[672,512]{1,0:T(8,128)(2,1)}, u32[]{:S(2)}, u32[]{:S(2)}) collective-permute-start(bf16[672,512]{1,0:T(8,128)(2,1)} %pad_maximum_fusion.2.refs_7_), channel_id=1, source_target_pairs={{0,4},{1,5},{2,6},{3,7},{4,0},{5,1},{6,2},{7,3},{8,12},{9,13},{10,... | collective-permute-start | bytes 2064392 | tf_op jit(solution)/shard_map/ppermute | solution.py:332
  51.7 4.7 %collective-permute-start.7 = (bf16[224,512]{1,0:T(8,128)(2,1)S(1)}, bf16[224,512]{1,0:T(8,128)(2,1)S(1)}, u32[]{:S(2)}, u32[]{:S(2)}) collective-permute-start(bf16[224,512]{1,0:T(8,128)(2,1)S(1)} %copy-done.13), channel_id=1, source_target_pairs={{0,1},{1,0},{2,3},{3,2},{4,5},{5,4},{6,7},{7,6},{8,9},{9,8},{10,11... | collective-permute-start | bytes 688136 | tf_op jit(solution)/shard_map/ppermute | solution.py:332
  51.7 4.1 %collective-permute-start.6 = (bf16[224,512]{1,0:T(8,128)(2,1)S(1)}, bf16[224,512]{1,0:T(8,128)(2,1)S(1)}, u32[]{:S(2)}, u32[]{:S(2)}) collective-permute-start(bf16[224,512]{1,0:T(8,128)(2,1)S(1)} %copy-done.11), channel_id=1, source_target_pairs={{0,1},{1,0},{2,3},{3,2},{4,5},{5,4},{6,7},{7,6},{8,9},{9,8},{10,11... | collective-permute-start | bytes 688136 | tf_op jit(solution)/shard_map/ppermute | solution.py:332
  53.6 12.6 %collective-permute-start.13 = (bf16[448,512]{1,0:T(8,128)(2,1)S(1)}, bf16[448,512]{1,0:T(8,128)(2,1)}, u32[]{:S(2)}, u32[]{:S(2)}) collective-permute-start(bf16[448,512]{1,0:T(8,128)(2,1)S(1)} %pad_maximum_fusion.4), channel_id=1, source_target_pairs={{0,2},{1,3},{2,0},{3,1},{4,6},{5,7},{6,4},{7,5},{8,10},{9,11},{10,... | collective-permute-start | bytes 1376264 | tf_op jit(solution)/shard_map/ppermute | solution.py:332
  54.4 12.3 %collective-permute-start.15 = (bf16[448,512]{1,0:T(8,128)(2,1)S(1)}, bf16[448,512]{1,0:T(8,128)(2,1)}, u32[]{:S(2)}, u32[]{:S(2)}) collective-permute-start(bf16[448,512]{1,0:T(8,128)(2,1)S(1)} %pad_maximum_fusion.5), channel_id=1, source_target_pairs={{0,4},{1,5},{2,6},{3,7},{4,0},{5,1},{6,2},{7,3},{8,12},{9,13},{10,... | collective-permute-start | bytes 1376264 | tf_op jit(solution)/shard_map/ppermute | solution.py:332
  55.8 12.2 %collective-permute-start.8 = (bf16[672,512]{1,0:T(8,128)(2,1)}, bf16[672,512]{1,0:T(8,128)(2,1)}, u32[]{:S(2)}, u32[]{:S(2)}) collective-permute-start(bf16[672,512]{1,0:T(8,128)(2,1)} %pad_maximum_fusion.2.refs_7_), channel_id=1, source_target_pairs={{0,1},{1,0},{2,3},{3,2},{4,5},{5,4},{6,7},{7,6},{8,9},{9,8},{10,11... | collective-permute-start | bytes 2064392 | tf_op jit(solution)/shard_map/ppermute | solution.py:332
  55.9 12.2 %collective-permute-start.11 = (bf16[672,512]{1,0:T(8,128)(2,1)}, bf16[672,512]{1,0:T(8,128)(2,1)}, u32[]{:S(2)}, u32[]{:S(2)}) collective-permute-start(bf16[672,512]{1,0:T(8,128)(2,1)} %collective-permute-done.9.refs_9_), channel_id=1, source_target_pairs={{0,1},{1,0},{2,3},{3,2},{4,5},{5,4},{6,7},{7,6},{8,9},{9,8},{10,11... | collective-permute-start | bytes 2064392 | tf_op jit(solution)/shard_map/ppermute | solution.py:332
  57.0 11.0 %collective-permute-start.12 = (bf16[672,512]{1,0:T(8,128)(2,1)}, bf16[672,512]{1,0:T(8,128)(2,1)}, u32[]{:S(2)}, u32[]{:S(2)}) collective-permute-start(bf16[672,512]{1,0:T(8,128)(2,1)} %collective-permute-done.10.refs_11_), channel_id=1, source_target_pairs={{0,1},{1,0},{2,3},{3,2},{4,5},{5,4},{6,7},{7,6},{8,9},{9,8},{10,11... | collective-permute-start | bytes 2064392 | tf_op jit(solution)/shard_map/ppermute | solution.py:332
  66.2 2.2 collective-permute-start.14
  66.7 2.3 collective-permute-start.16
  89.4 16.4 %collective-permute-start.17 = (bf16[2,32,1024]{2,1,0:T(8,128)(2,1)}, bf16[2,32,1024]{2,1,0:T(8,128)(2,1)}, u32[]{:S(2)}, u32[]{:S(2)}) collective-permute-start(bf16[2,32,1024]{2,1,0:T(8,128)(2,1)} %get-tuple-element.110), channel_id=1, source_target_pairs={{0,4},{4,8},{8,12},{12,16},{16,20},{20,24},{24,28},{28,0},{1,5},{5... | collective-permute-start | bytes 393224 | tf_op jit(solution)/shard_map/ppermute | solution.py:999
  89.9 15.9 %collective-permute-start.18 = (bf16[2,32,1024]{2,1,0:T(8,128)(2,1)}, bf16[2,32,1024]{2,1,0:T(8,128)(2,1)}, u32[]{:S(2)}, u32[]{:S(2)}) collective-permute-start(bf16[2,32,1024]{2,1,0:T(8,128)(2,1)} %get-tuple-element.109), channel_id=1, source_target_pairs={{0,28},{4,0},{8,4},{12,8},{16,12},{20,16},{24,20},{28,24},{1,29},{... | collective-permute-start | bytes 393224 | tf_op jit(solution)/shard_map/ppermute | solution.py:1000
  155.0 23.1 %collective-permute-start.19 = (f32[10752,128]{1,0:T(8,128)}, f32[10752,128]{1,0:T(8,128)}, u32[]{:S(2)}, u32[]{:S(2)}) collective-permute-start(f32[10752,128]{1,0:T(8,128)} %get-tuple-element.86), channel_id=1, source_target_pairs={{0,1},{1,0},{2,3},{3,2},{4,5},{5,4},{6,7},{7,6},{8,9},{9,8},{10,11... | collective-permute-start | bytes 16515080 | tf_op jit(solution)/shard_map/ppermute | solution.py:332
  173.4 9.5 %collective-permute-start.20 = (bf16[2,32,1024]{2,1,0:T(8,128)(2,1)}, bf16[2,32,1024]{2,1,0:T(8,128)(2,1)}, u32[]{:S(2)}, u32[]{:S(2)}) collective-permute-start(bf16[2,32,1024]{2,1,0:T(8,128)(2,1)} %get-tuple-element.88), channel_id=1, source_target_pairs={{0,28},{4,0},{8,4},{12,8},{16,12},{20,16},{24,20},{28,24},{1,29},{... | collective-permute-start | bytes 393224 | tf_op jit(solution)/shard_map/ppermute | solution.py:1016
  173.4 9.5 %collective-permute-start.21 = (bf16[2,32,1024]{2,1,0:T(8,128)(2,1)}, bf16[2,32,1024]{2,1,0:T(8,128)(2,1)}, u32[]{:S(2)}, u32[]{:S(2)}) collective-permute-start(bf16[2,32,1024]{2,1,0:T(8,128)(2,1)} %get-tuple-element.89), channel_id=1, source_target_pairs={{0,4},{4,8},{8,12},{12,16},{16,20},{20,24},{24,28},{28,0},{1,5},{5... | collective-permute-start | bytes 393224 | tf_op jit(solution)/shard_map/ppermute | solution.py:1017
  185.3 21.2 %collective-permute-start.22 = (bf16[3,2,448,128]{3,2,0,1:T(8,128)(2,1)S(1)}, bf16[3,2,448,128]{3,2,0,1:T(8,128)(2,1)}, u32[]{:S(2)}, u32[]{:S(2)}) collective-permute-start(bf16[3,2,448,128]{3,2,0,1:T(8,128)(2,1)S(1)} %slice_bitcast_fusion.4), channel_id=1, source_target_pairs={{0,2},{1,3},{2,0},{3,1},{4,6},{5,7},{6,4},{7,5},{8,10},{9,11},{10,... | collective-permute-start | bytes 2064392 | tf_op jit(solution)/shard_map/ppermute | solution.py:332
  186.6 20.0 %collective-permute-start.23 = (bf16[3,2,448,128]{3,2,0,1:T(8,128)(2,1)S(1)}, bf16[3,2,448,128]{3,2,0,1:T(8,128)(2,1)}, u32[]{:S(2)}, u32[]{:S(2)}) collective-permute-start(bf16[3,2,448,128]{3,2,0,1:T(8,128)(2,1)S(1)} %slice_bitcast_fusion.3), channel_id=1, source_target_pairs={{0,4},{1,5},{2,6},{3,7},{4,0},{5,1},{6,2},{7,3},{8,12},{9,13},{10,... | collective-permute-start | bytes 2064392 | tf_op jit(solution)/shard_map/ppermute | solution.py:332
  206.6 6.7 %collective-permute-start.24 = (f32[4736,128]{1,0:T(8,128)}, f32[4736,128]{1,0:T(8,128)}, u32[]{:S(2)}, u32[]{:S(2)}) collective-permute-start(f32[4736,128]{1,0:T(8,128)} %get-tuple-element.101), channel_id=1, source_target_pairs={{0,1},{1,0},{2,3},{3,2},{4,5},{5,4},{6,7},{7,6},{8,9},{9,8},{10,11... | collective-permute-start | bytes 7274504 | tf_op jit(solution)/shard_map/ppermute | solution.py:332
  208.4 10.7 %collective-permute-start.32 = (bf16[3,448,128]{2,1,0:T(8,128)(2,1)S(1)}, bf16[3,448,128]{2,1,0:T(8,128)(2,1)S(1)}, u32[]{:S(2)}, u32[]{:S(2)}) collective-permute-start(bf16[3,448,128]{2,1,0:T(8,128)(2,1)S(1)} %fusion.24), channel_id=1, source_target_pairs={{0,4},{1,5},{2,6},{3,7},{4,0},{5,1},{6,2},{7,3},{8,12},{9,13},{10,... | collective-permute-start | bytes 1032200 | tf_op jit(solution)/shard_map/ppermute | solution.py:332
  212.2 11.0 %collective-permute-start.33 = (bf16[3,448,128]{2,1,0:T(8,128)(2,1)S(1)}, bf16[3,448,128]{2,1,0:T(8,128)(2,1)S(1)}, u32[]{:S(2)}, u32[]{:S(2)}) collective-permute-start(bf16[3,448,128]{2,1,0:T(8,128)(2,1)S(1)} %fusion.25), channel_id=1, source_target_pairs={{0,2},{1,3},{2,0},{3,1},{4,6},{5,7},{6,4},{7,5},{8,10},{9,11},{10,... | collective-permute-start | bytes 1032200 | tf_op jit(solution)/shard_map/ppermute | solution.py:332
  215.8 14.7 %collective-permute-start.25 = (bf16[1472,128]{1,0:T(8,128)(2,1)S(1)}, bf16[1472,128]{1,0:T(8,128)(2,1)S(1)}, u32[]{:S(2)}, u32[]{:S(2)}) collective-permute-start(bf16[1472,128]{1,0:T(8,128)(2,1)S(1)} %pad_maximum_fusion.6), channel_id=1, source_target_pairs={{0,2},{1,3},{2,0},{3,1},{4,6},{5,7},{6,4},{7,5},{8,10},{9,11},{10,... | collective-permute-start | bytes 1130504 | tf_op jit(solution)/shard_map/ppermute | solution.py:332
  216.9 13.6 %collective-permute-start.27 = (bf16[1472,128]{1,0:T(8,128)(2,1)S(1)}, bf16[1472,128]{1,0:T(8,128)(2,1)S(1)}, u32[]{:S(2)}, u32[]{:S(2)}) collective-permute-start(bf16[1472,128]{1,0:T(8,128)(2,1)S(1)} %pad_maximum_fusion.7), channel_id=1, source_target_pairs={{0,4},{1,5},{2,6},{3,7},{4,0},{5,1},{6,2},{7,3},{8,12},{9,13},{10,... | collective-permute-start | bytes 1130504 | tf_op jit(solution)/shard_map/ppermute | solution.py:332
  230.9 11.6 %collective-permute-start.28 = (bf16[1024,128]{1,0:T(8,128)(2,1)S(1)}, bf16[1024,128]{1,0:T(8,128)(2,1)S(1)}, u32[]{:S(2)}, u32[]{:S(2)}) collective-permute-start(bf16[1024,128]{1,0:T(8,128)(2,1)S(1)} %pad_maximum_fusion.9), channel_id=1, source_target_pairs={{0,2},{1,3},{2,0},{3,1},{4,6},{5,7},{6,4},{7,5},{8,10},{9,11},{10,... | collective-permute-start | bytes 786440 | tf_op jit(solution)/shard_map/ppermute | solution.py:332
  232.0 10.6 %collective-permute-start.26 = (bf16[1024,128]{1,0:T(8,128)(2,1)S(1)}, bf16[1024,128]{1,0:T(8,128)(2,1)S(1)}, u32[]{:S(2)}, u32[]{:S(2)}) collective-permute-start(bf16[1024,128]{1,0:T(8,128)(2,1)S(1)} %pad_maximum_fusion.8), channel_id=1, source_target_pairs={{0,4},{1,5},{2,6},{3,7},{4,0},{5,1},{6,2},{7,3},{8,12},{9,13},{10,... | collective-permute-start | bytes 786440 | tf_op jit(solution)/shard_map/ppermute | solution.py:332
  233.3 15.1 %collective-permute-start.36 = (bf16[896,128]{1,0:T(8,128)(2,1)S(1)}, bf16[896,128]{1,0:T(8,128)(2,1)S(1)}, u32[]{:S(2)}, u32[]{:S(2)}) collective-permute-start(bf16[896,128]{1,0:T(8,128)(2,1)S(1)} %get-tuple-element.124), channel_id=1, source_target_pairs={{0,24},{1,25},{2,26},{3,27},{4,28},{5,29},{6,30},{7,31},{8,16},{9,... | collective-permute-start | bytes 688136 | tf_op jit(solution)/shard_map/ppermute | solution.py:552
  238.0 17.6 %collective-permute-start.35 = (bf16[896,128]{1,0:T(8,128)(2,1)}, bf16[896,128]{1,0:T(8,128)(2,1)}, u32[]{:S(2)}, u32[]{:S(2)}) collective-permute-start(bf16[896,128]{1,0:T(8,128)(2,1)} %get-tuple-element.123), channel_id=1, source_target_pairs={{0,16},{1,17},{2,18},{3,19},{4,20},{5,21},{6,22},{7,23},{8,24},{9,... | collective-permute-start | bytes 688136 | tf_op jit(solution)/shard_map/ppermute | solution.py:552
  240.0 15.7 %collective-permute-start.34 = (bf16[896,128]{1,0:T(8,128)(2,1)}, bf16[896,128]{1,0:T(8,128)(2,1)}, u32[]{:S(2)}, u32[]{:S(2)}) collective-permute-start(bf16[896,128]{1,0:T(8,128)(2,1)} %get-tuple-element.122), channel_id=1, source_target_pairs={{0,8},{1,9},{2,10},{3,11},{4,12},{5,13},{6,14},{7,15},{16,24},{17,... | collective-permute-start | bytes 688136 | tf_op jit(solution)/shard_map/ppermute | solution.py:552
  245.8 10.1 %collective-permute-start.31 = (bf16[896,128]{1,0:T(8,128)(2,1)}, bf16[896,128]{1,0:T(8,128)(2,1)}, u32[]{:S(2)}, u32[]{:S(2)}) collective-permute-start(bf16[896,128]{1,0:T(8,128)(2,1)} %get-tuple-element.118), channel_id=1, source_target_pairs={{7,31},{16,8},{24,0},{25,1},{26,2},{27,3},{28,4},{29,5},{30,6},{31... | collective-permute-start | bytes 688136 | tf_op jit(solution)/shard_map/ppermute | solution.py:552
  247.1 17.5 %collective-permute-start.30 = (bf16[896,128]{1,0:T(8,128)(2,1)}, bf16[896,128]{1,0:T(8,128)(2,1)}, u32[]{:S(2)}, u32[]{:S(2)}) collective-permute-start(bf16[896,128]{1,0:T(8,128)(2,1)} %get-tuple-element.119), channel_id=1, source_target_pairs={{15,31},{16,0},{17,1},{18,2},{19,3},{20,4},{21,5},{22,6},{23,7},{2... | collective-permute-start | bytes 688136 | tf_op jit(solution)/shard_map/ppermute | solution.py:552
  248.4 17.1 %collective-permute-start.29 = (bf16[896,128]{1,0:T(8,128)(2,1)}, bf16[896,128]{1,0:T(8,128)(2,1)}, u32[]{:S(2)}, u32[]{:S(2)}) collective-permute-start(bf16[896,128]{1,0:T(8,128)(2,1)} %get-tuple-element.117), channel_id=1, source_target_pairs={{0,8},{8,0},{9,1},{10,2},{11,3},{12,4},{13,5},{14,6},{15,7},{23,31}} | collective-permute-start | bytes 688136 | tf_op jit(solution)/shard_map/ppermute | solution.py:552
  267.8 24.3 %copy-start.8 = (f32[103920]{0:T(1024)}, f32[103920]{0:T(1024)S(1)}, u32[]{:S(2)}) copy-start(f32[103920]{0:T(1024)S(1)} %get-tuple-element.107) | copy-start | bytes 1247044
  267.8 24.2 %copy-start.9 = (f32[103920]{0:T(1024)}, f32[103920]{0:T(1024)S(1)}, u32[]{:S(2)}) copy-start(f32[103920]{0:T(1024)S(1)} %get-tuple-element.108) | copy-start | bytes 1247044
  270.6 21.5 %copy-start.18 = (f32[103920]{0:T(1024)S(1)}, f32[103920]{0:T(1024)}, u32[]{:S(2)}) copy-start(f32[103920]{0:T(1024)} %param.27) | copy-start | bytes 1247044
  271.4 1.1 collective-permute-start.37
  273.3 3.6 %collective-permute-start.38 = (f32[2,8]{1,0:T(2,128)S(1)}, f32[2,8]{1,0:T(2,128)S(1)}, u32[]{:S(2)}, u32[]{:S(2)}) collective-permute-start(f32[2,8]{1,0:T(2,128)S(1)} %fusion.47), channel_id=1, source_target_pairs={{0,2},{1,3},{2,0},{3,1},{4,6},{5,7},{6,4},{7,5},{8,10},{9,11},{10,... | collective-permute-start | bytes 200 | tf_op jit(solution)/shard_map/ppermute | solution.py:332
  276.9 3.6 %collective-permute-start.39 = (f32[2,8]{1,0:T(2,128)S(1)}, f32[2,8]{1,0:T(2,128)S(1)}, u32[]{:S(2)}, u32[]{:S(2)}) collective-permute-start(f32[2,8]{1,0:T(2,128)S(1)} %add.182), channel_id=1, source_target_pairs={{0,4},{1,5},{2,6},{3,7},{4,0},{5,1},{6,2},{7,3},{8,12},{9,13},{10,... | collective-permute-start | bytes 200 | tf_op jit(solution)/shard_map/ppermute | solution.py:332
  280.4 3.6 %collective-permute-start.40 = (f32[2,8]{1,0:T(2,128)S(1)}, f32[2,8]{1,0:T(2,128)S(1)}, u32[]{:S(2)}, u32[]{:S(2)}) collective-permute-start(f32[2,8]{1,0:T(2,128)S(1)} %add.183), channel_id=1, source_target_pairs={{0,8},{1,9},{2,10},{3,11},{4,12},{5,13},{6,14},{7,15},{8,0},{9,1},... | collective-permute-start | bytes 200 | tf_op jit(solution)/shard_map/ppermute | solution.py:332
  284.0 4.5 %collective-permute-start.41 = (f32[2,8]{1,0:T(2,128)S(1)}, f32[2,8]{1,0:T(2,128)S(1)}, u32[]{:S(2)}, u32[]{:S(2)}) collective-permute-start(f32[2,8]{1,0:T(2,128)S(1)} %add.184), channel_id=1, source_target_pairs={{0,16},{1,17},{2,18},{3,19},{4,20},{5,21},{6,22},{7,23},{8,24},{9,... | collective-permute-start | bytes 200 | tf_op jit(solution)/shard_map/ppermute | solution.py:332
  (22 other events, 135.1 us)
where the time goes:
time: 298 us; the launch traced here: 293 us
  Pallas kernels  129 us (43%)
  waiting for transfers between devices  53 us (18%)
  starting transfers between devices  47.5 us (16%)
  other arithmetic  33.9 us (11%)
  local copies, waits for them, and re-layouts  25.4 us (9%)
  between operations  4.31 us (1%)
    ppermute x32, waiting for transfers between devices, permute(): return lax.ppermute(x, AXES, [(d, d ^ mask) for d in range(count)])  43.2 us
    pallas_call x1, Pallas kernels, mlp(): pl.pallas_call(functools.partial(mlp_body, layout), out_shape=[shape((sam...  40.6 us
    ppermute x32, starting transfers between devices, permute(): return lax.ppermute(x, AXES, [(d, d ^ mask) for d in range(count)])  24.5 us
    pallas_call x1, Pallas kernels, encode_back(): pl.pallas_call(functools.partial(encode_back_body, layout), out_shape=[sh...  19.9 us
    pallas_call x1, Pallas kernels, attend_back(): kernel_call(attend_back_body, [shape((samples, nodes, 3 * D), BF), shape(...  18.1 us
    ppermute x6, starting transfers between devices, across_planes(): return lax.ppermute(x, AXES, pairs)  16 us
    pallas_call x1, Pallas kernels, encode(): kernel_call(encode_body, [shape((samples, nodes, D)), shape((samples, nod...  13.4 us
    pallas_call x2, Pallas kernels, unpack(): pl.pallas_call(functools.partial(unpack_body, plan, parts, sources, place...  12.1 us
  transfers between devices with their start and end apart: 42, of which 16 were waited for; matrix products, arithmetic and copies ran while one was open for 12% of the time, Pallas kernels for 21%

commit v1 on v0

--- a/solution.py
+++ b/solution.py
@@ -234,22 +234,33 @@
             ref[:, lanes] = stage[lane, pl.ds(c, ref.shape[0], stride=period), :].astype(BF)
 
 
-def unpack_body(plan, parts, sources, place_of, count, *refs):
+def unpack_body(plan, parts, sources, place_of, owner_of, count, *refs):
     me, pieces, refs = refs[0], refs[1 : count + 1], refs[count + 1 :]
     outs, (windows, stage, sems) = refs[: len(parts)], refs[len(parts) :]
+    here = me[0]
+    first = min(PARTS[p][0] for p in parts if p != "count")
+    last = max(PARTS[p][0] + PARTS[p][1] for p in parts if p not in ("count", "gains"))
+    used = {d for source in sources[first // 16 : last // 16] for d, _ in source}
+    if "gains" in parts:
+        used |= {d for d, _ in sources[ROW_GAIN // 16]}
+    low_used, high_used = min(used), max(used - {max(used)})
     copies = []
-
-    for k, (piece, at, slot, first, rows) in enumerate(plan):
+    for k, (piece, at, slot, to, rows) in enumerate(plan):
         copy = pltpu.make_async_copy(
-            pieces[piece].at[pl.ds(at, rows), :],
-            windows.at[slot, pl.ds(first, rows), :],
-            sems.at[k],
+            pieces[piece].at[pl.ds(at, rows), :], windows.at[slot, pl.ds(to, rows), :], sems.at[k]
         )
-        copy.start()
-        copies.append(copy)
-    for copy in copies:
-        copy.wait()
-    here = me[0]
+        owner = owner_of(here, slot)
+        needed = (owner >= low_used) & (owner <= high_used) | (owner == max(used))
+        if "count" in parts:
+            copy.start()
+        else:
+            pl.when(needed)(copy.start)
+        copies.append((copy, needed))
+    for copy, needed in copies:
+        if "count" in parts:
+            copy.wait()
+        else:
+            pl.when(needed)(copy.wait)
     window_rows = windows.shape[1]
 
     def read(d, off, rows):
@@ -274,13 +285,11 @@
                     :, lane * 128 : lane * 128 + 128
                 ]
 
-        if part == "gain":
+        if part == "gains":
             assemble(read, window_rows, sources, first, rows, staged)
             row = ROW_GAIN - first
             for lane in range(D // 128):
-                ref[:, lane * 128 : lane * 128 + 128] = stage[lane, row : row + 1, :] + jnp.zeros(
-                    (8, 128), F32
-                )
+                ref[:, lane * 128 : lane * 128 + 128] = stage[lane, row : row + 8, :]
         elif period == 1:
             assemble(read, window_rows, sources, first, rows, direct)
         else:
@@ -289,6 +298,11 @@
                 for lane in range(D // 128):
                     lanes = slice(lane * 128, lane * 128 + 128)
                     ref[:, lanes] = stage[lane, LEAD:ROW_QKV, :].astype(BF)
+            elif part == "dec":
+                for lane in range(D // 128):
+                    lanes = slice(lane * 128, lane * 128 + 128)
+                    row = ROW_DEC - first
+                    ref[:, lanes] = stage[lane, row : row + C_OUT, :].astype(BF)
             else:
                 wide(stage, ref, period)
 
@@ -296,22 +310,22 @@
 PARTS = {
     "enc": (0, ROW_QKV, 0, (C_IN, D)),
     "qkv": (ROW_QKV, 3 * D, 3, (D, 3 * D)),
-    "gain": (ROW_GAIN // 16 * 16, 16, 0, (8, D)),
     "out": (ROW_OUT, D, 1, (D, D)),
     "up": (ROW_UP, 4 * D, 4, (D, FF)),
     "down": (ROW_DOWN, FF, 1, (FF, D)),
-    "tail": (ROW_DEC, ROWS_ALL - ROW_DEC, 1, (ROWS_ALL - ROW_DEC, D)),
+    "dec": (ROW_DEC // 16 * 16, -(-ROW_GAIN // 16) * 16 - ROW_DEC // 16 * 16, 0, (C_OUT, D)),
+    "gains": (ROW_GAIN // 16 * 16, 16, 0, (8, D)),
 }
 
 
 def unpack(me, pieces, plan, parts, place_of, slots, rows, starts):
     sources = tile_sources(starts, rows)
     outs = [
-        shape((8, 128)) if p == "count" else shape(PARTS[p][3], F32 if p == "gain" else BF)
+        shape((8, 128)) if p == "count" else shape(PARTS[p][3], F32 if p == "gains" else BF)
         for p in parts
     ]
     return pl.pallas_call(
-        functools.partial(unpack_body, plan, parts, sources, place_of, len(pieces)),
+        functools.partial(unpack_body, plan, parts, sources, place_of, place_of, len(pieces)),
         out_shape=outs,
         in_specs=[pl.BlockSpec(memory_space=pltpu.SMEM)]
         + [pl.BlockSpec(memory_space=pl.ANY)] * len(pieces),
@@ -336,7 +350,7 @@
     return jnp.bitwise_xor(here, d)
 
 
-def gather_windows(window, first_work, second_work):
+def gather_windows(window, first_work, second_work, second_inputs, third_work, third_inputs):
     rows = window.shape[0]
     half = rows // 2
     pieces, plan = [], []
@@ -351,12 +365,14 @@
     others = [permute(window, m) for m in planes]
     by_x, by_y = permute(window, 2), permute(window, 4)
     first_done = first_work()
-    others, by_x, by_y, first_done = lax.optimization_barrier(
-        (jnp.concatenate(others), by_x, by_y, first_done)
+    others, by_x, by_y, first_done, second_inputs = lax.optimization_barrier(
+        (jnp.concatenate(others), by_x, by_y, first_done, second_inputs)
     )
     others_x, others_y = permute(others, 2), permute(others, 4)
-    second_done = second_work()
-    others_x, others_y, second_done = lax.optimization_barrier((others_x, others_y, second_done))
+    second_done = second_work(*second_inputs)
+    others_x, others_y, second_done, third_inputs = lax.optimization_barrier(
+        (others_x, others_y, second_done, third_inputs)
+    )
 
     def halves(near_part, far_part, first):
         far = [far_part[i * rows + first : i * rows + first + half] for i in range(3)]
@@ -364,6 +380,9 @@
 
     across_a = permute(halves(by_y, others_y, 0), 2)
     across_b = permute(halves(by_x, others_x, half), 4)
+    across_a, across_b, third_done = lax.optimization_barrier(
+        (across_a, across_b, third_work(*third_inputs))
+    )
     whole = [(0, 0, 0, rows)]
     stacked = [(i * rows, slot, 0, rows) for i, slot in enumerate(planes)]
     add(window, 0, whole)
@@ -374,12 +393,12 @@
     add(others_y, 4, stacked)
     add(across_a, 6, [(i * half, slot, 0, half) for i, slot in enumerate((0,) + planes)])
     add(across_b, 6, [(i * half, slot, half, half) for i, slot in enumerate((0,) + planes)])
-    return pieces, plan, first_done, second_done
-
-
-def encode_body(grid, w_enc, enc_m, w_qkv, gains, h0, qkv, high, low):
+    return pieces, plan, first_done, second_done, third_done
+
+
+def encode_body(grid, w_enc, enc_m, w_qkv, gains, h0, qkv, leading, last, high, low):
     samples, pixels = grid.shape[0], grid.shape[2]
-    nodes = h0.shape[1]
+    nodes, halo = h0.shape[1], last.shape[1]
     for s in range(samples):
 
         @pl.loop(0, pixels // 512, unroll=True)
@@ -399,13 +418,17 @@
             n1 = (hat * gains[0:1, :]).astype(BF)
             qkv[s, rows, :] = dot(n1, w_qkv[...]).astype(BF)
 
+        leading[s] = qkv[s, 0:halo, D:]
+        last[s] = qkv[s, nodes - halo :, D:]
+
 
 def encode(grid, w_enc, enc_m, w_qkv, gains):
     samples, pixels = grid.shape[0], grid.shape[2]
     nodes = enc_m.shape[0]
     return kernel_call(
         encode_body,
-        [shape((samples, nodes, D)), shape((samples, nodes, 3 * D), BF)],
+        [shape((samples, nodes, D)), shape((samples, nodes, 3 * D), BF)]
+        + [shape((samples, nodes // 16, 2 * D), BF)] * 2,
         [pltpu.VMEM((pixels, D), BF), pltpu.VMEM((pixels, D), BF)],
         nbytes=12 << 20,
         flops=8 << 30,
@@ -452,16 +475,17 @@
     def __init__(self, shard, devices, fast):
         self.devices = devices
         self.starts, self.win = window_plan(shard, devices)
-        self.rows = 4 * self.win
         self.begins = [(LEAD * D + d * shard) // 1024 * 8 for d in range(devices)]
         self.ends = [-(-(LEAD * D + (d + 1) * shard) // 1024) * 8 for d in range(devices)]
+        self.rows = -(-max(e - b for b, e in zip(self.begins, self.ends)) // 32) * 32
         self.small = 4 * (ROWS_ALL - ROW_DEC)
         first = (("out", ROW_OUT, 4 * D), ("up", ROW_UP, 16 * D), ("down", ROW_DOWN, 4 * FF))
         second = (("enc", ROW_ENC, 4 * C_IN), ("qkv", ROW_QKV, 12 * D), ("small", ROW_DEC, self.small))
         self.fast = fast
         if fast:
-            self.apart = 4 * (ROW_OUT - self.starts[8])
-            self.sizes = (12 * self.rows, 4 * self.rows + self.apart + self.small)
+            self.apart = 4 * ROW_OUT - self.begins[8]
+            extra = -(-(self.apart + self.small) // 32) * 32
+            self.sizes = (12 * self.rows, 4 * self.rows + extra)
         else:
             self.sizes = (sum(x[2] for x in first), sum(x[2] for x in second))
         self.plans = self.make(first, 1), self.make(second, 0)
@@ -478,16 +502,16 @@
                 plans[name].append((k, "both", 4 * self.rows + self.apart, 0, size))
                 k += 2
                 continue
-            for d, (lower, upper, start) in enumerate(zip(self.begins, self.ends, self.starts)):
+            for d, (lower, upper) in enumerate(zip(self.begins, self.ends)):
                 low, high = max(lower, 4 * row), min(upper, 4 * (row + size // 4))
                 if low >= high:
                     continue
                 if d == 8 and plane == 0:
-                    to = 4 * self.rows + low - 4 * start
+                    to = 4 * self.rows + low - lower
                     plans[name].append((k, "both", to, low - 4 * row, high - low))
                     k += 2
                 else:
-                    place = (d // 8 - plane) * 4 * self.rows + low - 4 * start
+                    place = (d // 8 - plane) * 4 * self.rows + low - lower
                     plans[name].append((k, d % 8, place, low - 4 * row, high - low))
                     k += 1
         return plans, k
@@ -526,10 +550,10 @@
             second[: 4 * (ROW_OUT - LEAD)],
             first,
             second[4 * (ROW_OUT - LEAD) :],
-            jnp.zeros((max(0, 4 * (layout.starts[-1] + layout.win - ROWS_ALL)), 128), F32),
+            jnp.zeros((max(0, layout.begins[-1] + layout.rows - 4 * ROWS_ALL), 128), F32),
         ]
     )
-    windows = jnp.concatenate([flat[4 * s : 4 * s + layout.rows] for s in layout.starts])
+    windows = jnp.concatenate([flat[b : b + layout.rows] for b in layout.begins])
     return lax.psum_scatter(windows, AXES, scatter_dimension=0, tiled=True)
 
 
@@ -552,27 +576,86 @@
     return lax.ppermute(x, AXES, pairs)
 
 
-def sum_rest(early, early_got, second, layout, me):
+def add_halves(layout, keep, other, got, sends):
+    half = layout.rows // 2
+    keep, other = keep.reshape(24, half, 128), other.reshape(24, half, 128)
+    steps = []
+    for out, (picks, source, _) in enumerate(sends):
+        for i, pick in enumerate(picks):
+            steps.append((out, i, pick, source))
+
+    def body(*refs):
+        keep_ref, other_ref = refs[:2]
+        gots, outs = refs[2 : 2 + len(got)], refs[2 + len(got) : 2 + len(got) + len(sends)]
+        slots, sems = refs[-2:]
+        copies = []
+        for k, (out, i, pick, source) in enumerate(steps):
+            pair = [
+                pltpu.make_async_copy(ref.at[pick], slots.at[2 * k + j], sems.at[2 * k + j])
+                for j, ref in enumerate((keep_ref, other_ref))
+            ]
+            for copy in pair:
+                copy.start()
+            copies.append(pair)
+        for k, (out, i, pick, source) in enumerate(steps):
+            for copy in copies[k]:
+                copy.wait()
+            value = slots[2 * k] + slots[2 * k + 1]
+            if source is not None:
+                which, at = source[0], source[1][i]
+                value = value + gots[which][at].astype(F32)
+            outs[out][i] = value.astype(outs[out].dtype)
+
+    hbm = pl.BlockSpec(memory_space=pl.ANY)
+    vmem = pl.BlockSpec(memory_space=pltpu.VMEM)
+    return pl.pallas_call(
+        body,
+        out_shape=[shape((len(p), half, 128), BF if sent else F32) for p, _, sent in sends],
+        in_specs=[hbm, hbm] + [vmem] * len(got),
+        out_specs=[vmem] * len(sends),
+        scratch_shapes=[
+            pltpu.VMEM((2 * len(steps), half, 128), F32),
+            pltpu.SemaphoreType.DMA((2 * len(steps),)),
+        ],
+        compiler_params=pltpu.CompilerParams(vmem_limit_bytes=58 << 20),
+        cost_estimate=pl.CostEstimate(
+            flops=0, bytes_accessed=len(steps) * half * 1536, transcendentals=0
+        ),
+    )(keep, other, *got)
+
+
+def first_send(keep, other, layout):
+    to_x = [(p * 4 + y * 2 + 1) * 2 for p in range(3) for y in range(2)]
+    to_y = [(p * 4 + 2 + x) * 2 + 1 for p in range(3) for x in range(2)]
+    return add_halves(layout, keep, other, (), [(to_x, None, True), (to_y, None, True)])
+
+
+def second_send(keep, other, got_a, got_b, layout):
+    sends = []
+    for which, (lower, stride) in enumerate(((0, 2), (1, 1))):
+        for far in range(2):
+            picks = [(p * 4 + far * stride) * 2 + lower for p in range(3)]
+            sends.append((picks, (which, [p * 2 + far for p in range(3)]), far == 1))
+    return add_halves(layout, keep, other, (got_a, got_b), sends)
+
+
+def sum_rest(kept, got, second, layout, me):
     rows = layout.rows
     half = rows // 2
     near, mine = me % 8, me // 8
 
-    late = second[0] + permute(second[1], 1)
-    early_a = early[:, :, 0, :half] + early_got[0].astype(F32)
-    early_b = early[:, 0, :, half:] + early_got[1].astype(F32)
-    early_a = early_a[:, 0] + permute(low(early_a[:, 1]), 4).astype(F32)
-    early_b = early_b[:, 0] + permute(low(early_b[:, 1]), 2).astype(F32)
-    planes = jnp.concatenate([early_a, early_b], axis=1)
+    other = permute(second[1], 1)
+    kept_a, kept_b = kept[0] + got[0].astype(F32), kept[1] + got[1].astype(F32)
 
     def plane(k):
-        return lax.dynamic_index_in_dim(
-            planes, jnp.maximum(jnp.bitwise_xor(mine, k) - 1, 0), 0, False
+        at = jnp.maximum(jnp.bitwise_xor(mine, k) - 1, 0)
+        return jnp.concatenate(
+            [lax.dynamic_index_in_dim(x, at, 0, False) for x in (kept_a, kept_b)]
         )
 
-    upper = plane(0)
-    for k in (1, 2, 3):
-        upper = upper + across_planes(low(plane(k)), lambda p, q: p > 0, k).astype(F32)
-
+    ups = [across_planes(low(plane(k)), lambda p, q: p > 0, k) for k in (1, 2, 3)]
+
+    late = second[0] + other
     apart = late[4 * rows :]
     late = late[: 4 * rows].reshape(2, 2, rows, 128)
     cut = apart.shape[0] // 2
@@ -585,9 +668,16 @@
     late_a, apart_a = add_packed(permute(packed(late_a[1], apart_a), 4), late_a[0], apart_a)
     late_b, apart_b = add_packed(permute(packed(late_b[1], apart_b), 2), late_b[0], apart_b)
     apart = jnp.concatenate([apart_a, apart_b])
-    lead, small = layout.apart, 4 * (ROW_DEC - layout.starts[31])
+    lead, small = layout.apart, 4 * ROW_DEC - layout.begins[31]
+    size = min(layout.small, rows - small)
     one = jnp.concatenate([apart[:lead], jnp.zeros((rows - lead, 128), F32)])
-    three = jnp.concatenate([jnp.zeros((small, 128), F32), apart[lead : lead + rows - small]])
+    three = jnp.concatenate(
+        [
+            jnp.zeros((small, 128), F32),
+            apart[lead : lead + size],
+            jnp.zeros((rows - small - size, 128), F32),
+        ]
+    )
     parts = jnp.stack([jnp.concatenate([late_a, late_b]), one, one, three])
 
     def part(k):
@@ -599,6 +689,9 @@
             low(part(k)), lambda p, q: p == 0 or (p, q) == (1, 0) or (p, q) == (3, 7), k
         )
         lower = lower + got.astype(F32)
+    upper = plane(0)
+    for up in ups:
+        upper = upper + up.astype(F32)
     row = lax.broadcasted_iota(jnp.int32, (rows, 1), 0)
     take = (mine == 0) | ((me == 8) & (row < lead)) | ((me == 31) & (row >= small))
     return jnp.where(take, lower, upper)
@@ -614,7 +707,7 @@
 
 def mlp_body(
     layout,
-    me, h0, attended, w_out, w_dec, gains, weight, levels, scale, w_up_hbm, w_down_hbm, dec_mt_hbm, targets_hbm,
+    me, h0, attended, w_out, w_dec, gains, weight, levels, counted, w_up_hbm, w_down_hbm, dec_mt_hbm, targets_hbm,
     dh1, d_dec, d_gains, loss, keep, send,
     h1, n2, upper, act, h2, n3, pred, d_pred, dm, du, d_y, total_out, d_out, d_up, d_down, w_up, w_down, dec_mt, targets_t, sems, in_sems,
 ):
@@ -629,6 +722,8 @@
     for load in loads:
         load.start()
     pixels = dec_mt.shape[1]
+    pred[...] = jnp.zeros(pred.shape, BF)
+    scale = (2.0 / counted[0:1, 0:1]) * (1.0 / 3.0)
     tile = 512
     tiles = nodes // tile
     for s in range(samples):
@@ -658,10 +753,9 @@
             hat, _ = norm(end)
             in_three = (hat * gains[2:3, :]).astype(BF)
             n3[flat, :] = in_three
-            y_t = dot(in_three, w_dec[...]).T
-            high, low = split(y_t[0:CP, :])
-            pred[s * CP : (s + 1) * CP, rows] = high
-            pred[(samples + s) * CP : (samples + s + 1) * CP, rows] = low
+            high, low = split(dot(in_three, w_dec[...]).T)
+            pred[s * CP : s * CP + C_OUT, rows] = high
+            pred[(samples + s) * CP : (samples + s) * CP + C_OUT, rows] = low
 
     loads[2].wait()
     loads[3].wait()
@@ -679,7 +773,7 @@
             misfit = y * (1.0 / 3.0) - targets_t[s, :, part]
             g = weight[s : s + 1, part] * levels[...] * misfit
             loss[...] += jnp.sum(g * misfit, axis=0, keepdims=True)
-            high, low = split(g * scale[0:1, 0:1])
+            high, low = split(g * scale)
             highs.append(high)
             lows.append(low)
         d_pred[...] += dot_nt(jnp.concatenate(highs + lows, axis=0), counts)
@@ -696,7 +790,7 @@
         def _(i):
             rows = pl.ds(pl.multiple_of(i * tile, tile), tile)
             flat = pl.ds(pl.multiple_of(s * nodes + i * tile, tile), tile)
-            d_part = d_y[rows, :]
+            d_part = d_y[rows, 0:C_OUT]
             d_dec[...] += dot_tn(n3[flat, :], d_part)
             grad = dot_nt(d_part, w_dec[...])
             hat, r = norm(h2[flat, :])
@@ -737,7 +831,7 @@
     copies("up", d_up, "wait")
 
 
-def mlp(me, h0, attended, w_out, w_up, w_down, w_dec, gains, dec_mt, targets_t, weight, levels, scale, layout):
+def mlp(me, h0, attended, w_out, w_up, w_down, w_dec, gains, dec_mt, targets_t, weight, levels, counted, layout):
     samples, nodes, _ = h0.shape
     rows = samples * nodes
     count = layout.plans[0][1]
@@ -748,7 +842,7 @@
         functools.partial(mlp_body, layout),
         out_shape=[
             shape((samples, nodes, D)),
-            shape((D, 128)),
+            shape((D, C_OUT)),
             shape((8, D)),
             shape((1, 512)),
             shape((layout.sizes[0], 128)),
@@ -781,7 +875,7 @@
         ],
         compiler_params=pltpu.CompilerParams(vmem_limit_bytes=60 << 20),
         cost_estimate=pl.CostEstimate(flops=16 << 30, bytes_accessed=24 << 20, transcendentals=0),
-    )(me, h0, attended, w_out, w_dec, gains, weight, levels, scale, w_up, w_down, dec_mt, targets_t)
+    )(me, h0, attended, w_out, w_dec, gains, weight, levels, counted, w_up, w_down, dec_mt, targets_t)
 
 
 def attend_back_body(
@@ -847,12 +941,11 @@
     )(qkv, before, after, log_c, dh1, w_out)
 
 
-def encode_back_body(
+def node_back_body(
     layout,
-    me, grid, w_enc, w_qkv, gains, enc_mt, h0, dh1, d_in, d_rims, from_lower, from_upper,
-    d_small,
-    keep, send,
-    dqkv, n1, both, total_enc, d_gain, d_enc, d_qkv, small, sems,
+    me, w_qkv, gains, h0, dh1, d_in, d_rims, from_lower, from_upper, d_dec, d_gains,
+    both, keep, send,
+    dqkv, n1, d_gain, d_qkv, small, sems,
 ):
     samples, nodes, _ = h0.shape
     here = me[0]
@@ -862,11 +955,8 @@
             here, layout.rows, layout.plans[1][0][name], source, keep, send, sems, action
         )
 
-    small[...] = d_small[...]
-    pixels = grid.shape[2]
     halo = from_lower.shape[1]
-    d_gain[...] = jnp.zeros(d_gain.shape, F32)
-    total_enc[...] = jnp.zeros(total_enc.shape, F32)
+    d_gain[...] = d_gains[...]
     for s in range(samples):
         base = s * nodes
         dqkv[base : base + nodes, :] = d_in[s]
@@ -874,67 +964,95 @@
         dqkv[base : base + halo, D:] = low_rim.astype(BF)
         high_rim = d_rims[s, 1] + from_upper[s].astype(F32)
         dqkv[base + nodes - halo : base + nodes, D:] = high_rim.astype(BF)
-        for i in range(nodes // 256):
-            rows = slice(i * 256, (i + 1) * 256)
-            flat = slice(base + i * 256, base + (i + 1) * 256)
-            hat, r = norm(h0[s, rows, :])
-            n1[flat, :] = (hat * gains[0:1, :]).astype(BF)
-            grad = dot_nt(dqkv[flat, :], w_qkv[...])
-            d_gain[0:1, :] += jnp.sum(grad * hat, axis=0, keepdims=True)
-            d_start = dh1[s, rows, :] + norm_back(grad, gains[0:1, :], hat, r)
-            high, low = split(d_start * 0.25)
-            both[rows, 0:D] = high
-            both[rows, D:] = low
+        flat = slice(base, base + nodes)
+        hat, r = norm(h0[s])
+        n1[flat, :] = (hat * gains[0:1, :]).astype(BF)
+        grad = dot_nt(dqkv[flat, :], w_qkv[...])
+        d_gain[0:1, :] += jnp.sum(grad * hat, axis=0, keepdims=True)
+        d_start = dh1[s] + norm_back(grad, gains[0:1, :], hat, r)
+        high, low = split(d_start * 0.25)
+        both[s, :, 0:D] = high
+        both[s, :, D:] = low
+    small[0 : 4 * C_OUT, :] = d_dec[...]
+    small[4 * C_OUT :, :] = jnp.zeros((small.shape[0] - 4 * C_OUT, 128), F32)
+    for k in range(3):
+        for lane in range(D // 128):
+            row = 4 * (C_OUT + k) + lane
+            small[row : row + 1, :] = d_gain[k : k + 1, lane * 128 : lane * 128 + 128]
+    copies("small", small, "start")
+    for c in range(3):
+        put_flat(d_qkv, dot_tn(n1[...], dqkv[:, c * D : (c + 1) * D]), 4 * c, 12)
+    copies("qkv", d_qkv, "start")
+    copies("small", small, "wait")
+    copies("qkv", d_qkv, "wait")
+
+
+def node_back(me, w_qkv, gains, h0, dh1, d_in, d_rims, from_lower, from_upper, d_dec, d_gains, layout):
+    samples, nodes, _ = h0.shape
+    rows = samples * nodes
+    vmem = pl.BlockSpec(memory_space=pltpu.VMEM)
+    hbm = pl.BlockSpec(memory_space=pl.ANY)
+    return pl.pallas_call(
+        functools.partial(node_back_body, layout),
+        out_shape=[
+            shape((samples, nodes, 2 * D), BF),
+            shape((layout.sizes[1], 128)),
+            shape((layout.sizes[1] if layout.fast else 8, 128)),
+        ],
+        in_specs=[pl.BlockSpec(memory_space=pltpu.SMEM)] + [vmem] * 10,
+        out_specs=[vmem, hbm, hbm],
+        scratch_shapes=[
+            pltpu.VMEM((rows, 3 * D), BF),
+            pltpu.VMEM((rows, D), BF),
+            pltpu.VMEM((8, D), F32),
+            pltpu.VMEM((12 * D, 128), F32),
+            pltpu.VMEM((layout.small, 128), F32),
+            pltpu.SemaphoreType.DMA((layout.plans[1][1],)),
+        ],
+        compiler_params=pltpu.CompilerParams(vmem_limit_bytes=58 << 20),
+        cost_estimate=pl.CostEstimate(flops=8 << 30, bytes_accessed=16 << 20, transcendentals=0),
+    )(me, w_qkv, gains, h0, dh1, d_in, d_rims, from_lower, from_upper, d_dec, d_gains)
+
+
+def pixel_back_body(layout, me, grid, w_enc, enc_mt, both, keep_in, send_in, keep, send, total, d_enc, sems):
+    samples, _, pixels = grid.shape
+    total[...] = jnp.zeros(total.shape, F32)
+    for s in range(samples):
 
         @pl.loop(0, pixels // 512, unroll=True)
         def _(i):
             rows = pl.ds(pl.multiple_of(i * 512, 512), 512)
             x_t = grid[s, :, rows]
             pre = dot_tn(x_t, w_enc[...])
-            spread2 = dot(enc_mt[rows, :], both[...])
+            spread2 = dot(enc_mt[rows, :], both[s])
             spread = spread2[:, 0:D] + spread2[:, D:]
             d_pre = (spread * slope(pre, sigmoid(pre))).astype(BF)
-            total_enc[...] += dot(x_t, d_pre)
-
-    for c in range(3):
-        put_flat(d_qkv, dot_tn(n1[...], dqkv[:, c * D : (c + 1) * D]), 4 * c, 12)
-    copies("qkv", d_qkv, "start")
-    put_flat(d_enc, total_enc[...], 0, 4)
-    for lane in range(D // 128):
-        row = 4 * C_OUT + lane
-        small[row : row + 1, :] = d_gain[0:1, lane * 128 : lane * 128 + 128]
+            total[...] += dot(x_t, d_pre)
+
+    put_flat(d_enc, total[...], 0, 4)
     for action in ("start", "wait"):
-        copies("enc", d_enc, action)
-        copies("small", small, action)
-        if action == "wait":
-            copies("qkv", d_qkv, action)
-
-
-def encode_back(me, grid, w_enc, w_qkv, gains, enc_mt, h0, dh1, d_in, d_rims, from_lower, from_upper,
-                d_small, layout):
-    samples, nodes, _ = h0.shape
-    rows = samples * nodes
+        window_copies(
+            me[0], layout.rows, layout.plans[1][0]["enc"], d_enc, keep, send, sems, action
+        )
+
+
+def pixel_back(me, grid, w_enc, enc_mt, both, keep, send, layout):
     vmem = pl.BlockSpec(memory_space=pltpu.VMEM)
     hbm = pl.BlockSpec(memory_space=pl.ANY)
     return pl.pallas_call(
-        functools.partial(encode_back_body, layout),
-        out_shape=[shape((layout.sizes[1], 128)), shape((layout.sizes[1] if layout.fast else 8, 128))],
-        in_specs=[pl.BlockSpec(memory_space=pltpu.SMEM)] + [vmem] * 12,
+        functools.partial(pixel_back_body, layout),
+        out_shape=[shape(keep.shape), shape(send.shape)],
+        in_specs=[pl.BlockSpec(memory_space=pltpu.SMEM)] + [vmem] * 4 + [hbm] * 2,
         out_specs=[hbm, hbm],
+        input_output_aliases={5: 0, 6: 1},
         scratch_shapes=[
-            pltpu.VMEM((rows, 3 * D), BF),
-            pltpu.VMEM((rows, D), BF),
-            pltpu.VMEM((nodes, 2 * D), BF),
             pltpu.VMEM((C_IN, D), F32),
-            pltpu.VMEM((8, D), F32),
             pltpu.VMEM((4 * C_IN, 128), F32),
-            pltpu.VMEM((12 * D, 128), F32),
-            pltpu.VMEM(d_small.shape, F32),
             pltpu.SemaphoreType.DMA((layout.plans[1][1],)),
         ],
         compiler_params=pltpu.CompilerParams(vmem_limit_bytes=58 << 20),
-        cost_estimate=pl.CostEstimate(flops=12 << 30, bytes_accessed=24 << 20, transcendentals=0),
-    )(me, grid, w_enc, w_qkv, gains, enc_mt, h0, dh1, d_in, d_rims, from_lower, from_upper, d_small)
+        cost_estimate=pl.CostEstimate(flops=8 << 30, bytes_accessed=12 << 20, transcendentals=0),
+    )(me, grid, w_enc, enc_mt, both, keep, send)
 
 
 def ring(axis, distance):
@@ -956,8 +1074,6 @@
     shard = params.shape[0]
     devices = lax.axis_size(AXES)
     me = lax.axis_index(AXES)
-    nodes = neighbours.shape[0]
-    halo = nodes // 16
     fast = (lax.axis_size("patch"), lax.axis_size("dp")) == (8, 4)
     layout = Layout(shard, devices, fast)
     starts, win = layout.starts, layout.win
@@ -973,73 +1089,81 @@
     levels = jnp.pad(level_weight, (0, CP - C_OUT)).reshape(CP, 1)
     pixels = dec_index.shape[0]
     first_work = lambda: count_encoder(enc_index, pixels)
-    positions = me * shard + lax.iota(jnp.int32, shard)
-    bounds = segment_bounds() + [(-1, -1)]
-    lower = jnp.array([x for x, _ in bounds], jnp.int32)[:, None]
-    upper = jnp.array([x for _, x in bounds], jnp.int32)[:, None]
-    member = ((positions >= lower) & (positions < upper)).astype(F32)
-    second_work = lambda: (count_rest(dec_index, neighbours, targets), weight, levels, member)
+    local_count = count.astype(F32)
+
+    def second_work(dec_index, neighbours, targets):
+        return count_rest(dec_index, neighbours, targets), weight, levels
+
+    def third_work(params):
+        positions = me * shard + lax.iota(jnp.int32, shard)
+        bounds = segment_bounds() + [(-1, -1)]
+        lower = jnp.array([x for x, _ in bounds], jnp.int32)[:, None]
+        upper = jnp.array([x for _, x in bounds], jnp.int32)[:, None]
+        member = ((positions >= lower) & (positions < upper)).astype(F32)
+        return member, jnp.sum(member * (params * params)[None, :], axis=1)
+
+    second_inputs, third_inputs = (dec_index, neighbours, targets), (params,)
     if fast:
-        pieces, plan, first_done, second_done = gather_windows(payload, first_work, second_work)
+        pieces, plan, first_done, second_done, third_done = gather_windows(
+            payload, first_work, second_work, second_inputs, third_work, third_inputs
+        )
         place_of = place_by_xor
     else:
         everything = lax.all_gather(payload, AXES, axis=0, tiled=False)
         pieces = [everything.reshape(devices * win, D)]
         plan = [(0, d * win, d, 0, win) for d in range(devices)]
         place_of = lambda here, d: d
-        first_done, second_done = first_work(), second_work()
+        first_done, second_done = first_work(), second_work(*second_inputs)
+        third_done = third_work(*third_inputs)
+    member, old_sums = third_done
     enc_m, enc_mt = first_done
-    (dec_mt, log_c, targets_t), weight, levels, member = second_done
+    (dec_mt, log_c, targets_t), weight, levels = second_done
     grid = jnp.swapaxes(grid, 1, 2)
 
-    w_enc, w_qkv, head = unpack(
-        place, pieces, plan, ("enc", "qkv", "gain"), place_of, devices, win, starts
-    )
-    h0, qkv = encode(grid, w_enc, enc_m, w_qkv, head)
-    before = lax.ppermute(qkv[:, nodes - halo :, D:], "patch", ring("patch", 1))
-    after = lax.ppermute(qkv[:, :halo, D:], "patch", ring("patch", -1))
-    w_out, w_up, w_down, tail, counted = unpack(
-        place, pieces, plan, ("out", "up", "down", "tail", "count"), place_of, devices, win, starts
-    )
-    w_dec = jnp.pad(tail[:C_OUT].reshape(D, C_OUT), ((0, 0), (0, 128 - C_OUT)))
-    gains = jnp.pad(tail[C_OUT : C_OUT + 3].astype(F32), ((0, 5), (0, 0)))
-    count_total = counted[0, 0]
+    w_enc, w_qkv, gains = unpack(
+        place, pieces, plan, ("enc", "qkv", "gains"), place_of, devices, win, starts
+    )
+    h0, qkv, leading, last = encode(grid, w_enc, enc_m, w_qkv, gains)
+    before = lax.ppermute(last, "patch", ring("patch", 1))
+    after = lax.ppermute(leading, "patch", ring("patch", -1))
+    w_out, w_up, w_down, w_dec, counted = unpack(
+        place, pieces, plan, ("out", "up", "down", "dec", "count"), place_of, devices, win, starts
+    )
+    w_dec = w_dec.reshape(D, C_OUT)
     attended = attend(qkv, before, after, log_c)
-    scale = 2.0 / counted * (1.0 / 3.0)
     dh1, d_dec, d_gains, loss_rows, keep, send = mlp(
         place, h0, attended, w_out, w_up, w_down, w_dec, gains, dec_mt, targets_t, weight, levels,
-        scale, layout,
-    )
+        counted, layout,
+    )
+    back = attend_back(qkv, before, after, log_c, dh1, w_out)
     if fast:
-        summed = keep + permute(send, 1)
-    d_qkv, d_rims, d_before, d_after = attend_back(qkv, before, after, log_c, dh1, w_out)
+        other = permute(send, 1)
+        other, back = lax.optimization_barrier((other, back))
+    d_qkv, d_rims, d_before, d_after = back
     from_upper = lax.ppermute(d_before, "patch", ring("patch", -1))
     from_lower = lax.ppermute(d_after, "patch", ring("patch", 1))
-    d_small = jnp.concatenate(
-        [
-            d_dec[:, :C_OUT].reshape(4 * C_OUT, 128),
-            jnp.zeros((4, 128), F32),
-            d_gains[1:3].reshape(8, 128),
-            jnp.zeros((4 * (ROWS_ALL - ROW_END), 128), F32),
-        ]
-    )
+    d_dec = d_dec.reshape(4 * C_OUT, 128)
     if fast:
-        summed, d_qkv, from_upper, from_lower, d_small = lax.optimization_barrier(
-            (summed, d_qkv, from_upper, from_lower, d_small)
+        send_a, send_b = first_send(keep, other, layout)
+        got = permute(send_a, 2), permute(send_b, 4)
+        send_a, send_b, d_dec, from_upper, from_lower = lax.optimization_barrier(
+            (send_a, send_b, d_dec, from_upper, from_lower)
         )
-        half = layout.rows // 2
-        early = summed.reshape(3, 2, 2, layout.rows, 128)
-        got = permute(low(early[:, :, 1, :half]), 2), permute(low(early[:, 1, :, half:]), 4)
-    second = encode_back(
-        place, grid, w_enc, w_qkv, gains, enc_mt, h0, dh1, d_qkv, d_rims, from_lower, from_upper,
-        d_small, layout,
+    second = node_back(
+        place, w_qkv, gains, h0, dh1, d_qkv, d_rims, from_lower, from_upper, d_dec, d_gains, layout
     )
     if fast:
         second, got = lax.optimization_barrier((second, got))
-        grad_window = sum_rest(early, got, second, layout, me)
+        keep_a, send_a, keep_b, send_b = second_send(keep, other, *got, layout)
+        got = permute(send_a, 4), permute(send_b, 2)
+        second, send_a, send_b = lax.optimization_barrier((second, send_a, send_b))
+    second = pixel_back(place, grid, w_enc, enc_mt, *second, layout)
+    if fast:
+        second, got = lax.optimization_barrier((second, got))
+        grad_window = sum_rest((keep_a, keep_b), got, second, layout, me)
     else:
         grad_window = sum_flat(keep, second[0], layout)
-    grad = lax.dynamic_slice(grad_window.reshape(-1), (shift,), (shard,))
+    grad = lax.dynamic_slice(grad_window.reshape(-1), (begin - begin // 1024 * 1024,), (shard,))
 
     new_first = BETA_ONE * first_moment + (1.0 - BETA_ONE) * grad
     new_second = BETA_TWO * second_moment + (1.0 - BETA_TWO) * grad * grad
@@ -1049,17 +1173,16 @@
         / (jnp.sqrt(new_second / (1.0 - BETA_TWO**STEP)) + LAMB_EPS)
         + DECAY * params
     )
-    both = jnp.stack([params * params, update * update])
-    sums = jnp.sum(member[None] * both[:, None, :], axis=2)
-    loss_at = (jnp.arange(2)[:, None] == 0) & (jnp.arange(8)[None, :] == 7)
-    sums = jnp.where(loss_at, jnp.sum(loss_rows), sums)
+    sums = jnp.stack([old_sums, jnp.sum(member * (update * update)[None, :], axis=1)])
+    own = jnp.stack([jnp.sum(loss_rows), local_count])[:, None]
+    sums = jnp.where(jnp.arange(8)[None, :] == 7, own, sums)
     totals = sum_everywhere(sums, fast)
     norms = jnp.sqrt(totals[:, :7])
     step_ratio = jnp.sum(member[:7] * (norms[0] / norms[1])[:, None], axis=0)
     new_params = params - RATE * step_ratio * update
     new_average = EMA_KEEP * average + (1.0 - EMA_KEEP) * new_params
     return (
-        jnp.stack([totals[0, 7], count_total]),
+        totals[:, 7],
         norms,
         new_params,
         new_first,

time: 298 us -> 274 us (0.919)
  other arithmetic: 33.9 us -> 17.3 us
  waiting for transfers between devices: 53 us -> 44.8 us
  local copies, waits for them, and re-layouts: 25.4 us -> 18.8 us
  starting transfers between devices: 47.5 us -> 52.8 us
  Pallas kernels: 129 us -> 132 us
    pallas_call x1 -> x4, Pallas kernels: 19.9 us -> 33.2 us  [the longest x1 13 us: pixel_back(): pl.pallas_call(functools.partial(pixel_back_body, layout), out_shape=[sha...]
    pallas_call x1, Pallas kernels: 40.6 us -> 31.4 us  [mlp(): pl.pallas_call(functools.partial(mlp_body, layout), out_shape=[shape((sam...]
    ppermute x32, waiting for transfers between devices: 43.2 us -> 34.4 us  [permute(): return lax.ppermute(x, AXES, [(d, d ^ mask) for d in range(count)])]
    add x7 -> x4, other arithmetic: 10.9 us -> 5.09 us  [the longest x1 1.87 us: sum_rest(): late = second[0] + other]
    ppermute x32, starting transfers between devices: 24.5 us -> 29.7 us  [permute(): return lax.ppermute(x, AXES, [(d, d ^ mask) for d in range(count)])]
    slice x7 -> x2, local copies, waits for them, and re-layouts: 5.8 us -> 0.71 us  [the longest x1 0.69 us: per_device(): return (totals[:, 7], norms, new_params, new_first, new_second, new_average)]
    unnamed x58 -> x89, local copies, waits for them, and re-layouts: 9.31 us -> 5.9 us
    optimization_barrier x1 -> x2, local copies, waits for them, and re-layouts: 1.36 us -> 4.37 us  [the longest x1 3.65 us: gather_windows(): lax.optimization_barrier((jnp.concatenate(others), by_x, by_y, first_done...]
  transfers between devices with their start and end apart: 42 -> 42, of which waited for: 16 -> 19; matrix products, arithmetic and copies ran while one was open for 12% -> 7% of each run, Pallas kernels for 21% -> 26%
where the time goes in v1:
time: 274 us; the launch traced here: 271 us
  Pallas kernels  132 us (48%)
  starting transfers between devices  52.8 us (19%)
  waiting for transfers between devices  44.8 us (16%)
  local copies, waits for them, and re-layouts  18.8 us (7%)
  other arithmetic  17.3 us (6%)
  between operations  5.19 us (2%)
    ppermute x32, waiting for transfers between devices, permute(): return lax.ppermute(x, AXES, [(d, d ^ mask) for d in range(count)])  34.4 us
    pallas_call x1, Pallas kernels, mlp(): pl.pallas_call(functools.partial(mlp_body, layout), out_shape=[shape((sam...  31.4 us
    ppermute x32, starting transfers between devices, permute(): return lax.ppermute(x, AXES, [(d, d ^ mask) for d in range(count)])  29.7 us
    pallas_call x1, Pallas kernels, attend_back(): kernel_call(attend_back_body, [shape((samples, nodes, 3 * D), BF), shape(...  17.9 us
    ppermute x6, starting transfers between devices, across_planes(): return lax.ppermute(x, AXES, pairs)  15.7 us
    pallas_call x1, Pallas kernels, encode(): kernel_call(encode_body, [shape((samples, nodes, D)), shape((samples, nod...  13.5 us
    pallas_call x1, Pallas kernels, pixel_back(): pl.pallas_call(functools.partial(pixel_back_body, layout), out_shape=[sha...  13 us
    pallas_call x1, Pallas kernels, node_back(): pl.pallas_call(functools.partial(node_back_body, layout), out_shape=[shap...  11.1 us
  transfers between devices with their start and end apart: 42, of which 19 were waited for; matrix products, arithmetic and copies ran while one was open for 7% of the time, Pallas kernels for 26%

profile of v1, /device:TPU:0, one launch (start us, length us, event | category | flops | bytes accessed | tf_op | source)
XLA Modules:
  0.0 270.5 jit_solution(8362132009620673214)
XLA Ops:
  5.8 2.0 dynamic_update_slice.6
  8.3 3.1 %collective-permute-start.1 = (bf16[224,512]{1,0:T(8,128)(2,1)S(1)}, bf16[224,512]{1,0:T(8,128)(2,1)S(1)}, u32[]{:S(2)}, u32[]{:S(2)}) collective-permute-start(bf16[224,512]{1,0:T(8,128)(2,1)S(1)} %reshape.94.refs_1_), channel_id=1, source_target_pairs={{0,8},{1,9},{2,10},{3,11},{4,12},{5,13},{6,14},{7,15},{8,0},{9,1},... | collective-permute-start | bytes 688136 | tf_op jit(solution)/shard_map/ppermute | solution.py:346
  11.4 2.6 collective-permute-start.2
  14.0 1.7 collective-permute-start.4
  15.7 1.5 collective-permute-start.5
  17.2 1.5 copy.29.enc
  18.8 7.8 %shard_map.190 = (bf16[512,2048]{1,0:T(8,128)(2,1)}, bf16[2048,512]{1,0:T(8,128)(2,1)}) custom-call(s32[512,4]{1,0:T(8,128)} %copy.29.enc, s32[4,512]{1,0:T(4,128)} %bitcast.90), custom_call_target="tpu_custom_call" | custom-call | flops 536870912 | bytes 5242880 | tf_op jit(solution)/shard_map/pallas_call | solution.py:174
  26.5 4.1 %collective-permute-done.2 = bf16[224,512]{1,0:T(8,128)(2,1)S(1)} collective-permute-done((bf16[224,512]{1,0:T(8,128)(2,1)S(1)}, bf16[224,512]{1,0:T(8,128)(2,1)S(1)}, u32[]{:S(2)}, u32[]{:S(2)}) %collective-permute-start.2) | collective-permute-done | bytes 229408 | tf_op jit(solution)/shard_map/ppermute | solution.py:346
  30.7 1.6 collective-permute-start.10
  32.3 1.5 collective-permute-start.9
  35.9 3.6 %copy.30.targets = f32[2,2048,84]{2,1,0:T(8,128)} copy(f32[2,2048,84]{1,0,2:T(2,128)} %param.16) | data formatting | bytes 2752512 | tf_op jit(solution)/shard_map/optimization_barrier | solution.py:368
  39.6 8.7 %shard_map.191 = (bf16[512,2048]{1,0:T(8,128)(2,1)}, f32[576,512]{1,0:T(8,128)}, f32[2,96,2048]{2,1,0:T(8,128)}) custom-call(s32[3,2048]{1,0:T(4,128)} %bitcast.88, s32[16,512]{1,0:T(8,128)} %bitcast.89, f32[2,2048,84]{2,1,0:T(8,128)} %copy.30.targets), custom_call_target="tpu_custom_call" | custom-call | flops 536870912 | bytes 8388608 | tf_op jit(solution)/shard_map/pallas_call | solution.py:185
  51.3 6.4 %collective-permute-done.14.refs_15_ = bf16[448,512]{1,0:T(8,128)(2,1)S(1)} collective-permute-done((bf16[448,512]{1,0:T(8,128)(2,1)S(1)}, bf16[448,512]{1,0:T(8,128)(2,1)S(1)}, u32[]{:S(2)}, u32[]{:S(2)}) %collective-permute-start.14) | collective-permute-done | bytes 458784 | tf_op jit(solution)/shard_map/ppermute | solution.py:346
  58.7 1.6 select_reduce_fusion
  63.7 3.8 %shard_map.192 = (bf16[264,512]{1,0:T(8,128)(2,1)}, bf16[512,1536]{1,0:T(8,128)(2,1)}, f32[8,512]{1,0:T(8,128)}) custom-call(s32[1]{0:T(128)} %bitcast.refs_0_.me, bf16[224,512]{1,0:T(8,128)(2,1)} %copy-done.13, bf16[224,512]{1,0:T(8,128)(2,1)} %collective-permute-done.refs_2_, bf16[224,512]{1,0:T(8,128)(2,1)} %copy-done.20, bf16[224,512]{1,0:T(8,128)(2,1)} %copy-done.24, ...), custom_call_target="tpu_custom_call" | custom-call | bytes 14680064 | tf_op jit(solution)/shard_map/pallas_call | solution.py:327
  67.5 13.5 %shard_map.193 = (f32[2,512,512]{2,1,0:T(8,128)}, bf16[2,512,1536]{2,1,0:T(8,128)(2,1)}, bf16[2,32,1024]{2,1,0:T(8,128)(2,1)}, bf16[2,32,1024]{2,1,0:T(8,128)(2,1)}) custom-call(bf16[2,264,2048]{2,1,0:T(8,128)(2,1)} %bitcast.97, bf16[264,512]{1,0:T(8,128)(2,1)} %get-tuple-element.100.w_enc, bf16[512,2048]{1,0:T(8,128)(2,1)} %get-tuple-element.101.enc_m, ...), custom_call_target="tpu_custom_call" | custom-call | flops 8589934592 | bytes 12582912 | tf_op jit(solution)/shard_map/pallas_call | solution.py:428
  82.0 4.0 %collective-permute-start.18 = (bf16[2,32,1024]{2,1,0:T(8,128)(2,1)}, bf16[2,32,1024]{2,1,0:T(8,128)(2,1)}, u32[]{:S(2)}, u32[]{:S(2)}) collective-permute-start(bf16[2,32,1024]{2,1,0:T(8,128)(2,1)} %get-tuple-element.107), channel_id=1, source_target_pairs={{0,28},{4,0},{8,4},{12,8},{16,12},{20,16},{24,20},{28,24},{1,29},{... | collective-permute-start | bytes 393224 | tf_op jit(solution)/shard_map/ppermute | solution.py:1128
  86.7 6.9 %shard_map.195 = (bf16[512,512]{1,0:T(8,128)(2,1)}, bf16[512,2048]{1,0:T(8,128)(2,1)}, bf16[2048,512]{1,0:T(8,128)(2,1)}, bf16[84,512]{1,0:T(8,128)(2,1)}, f32[8,128]{1,0:T(8,128)}) custom-call(s32[1]{0:T(128)} %bitcast.refs_0_.me, bf16[224,512]{1,0:T(8,128)(2,1)} %copy-done.13, bf16[224,512]{1,0:T(8,128)(2,1)} %collective-permute-done.refs_2_, ...), custom_call_target="tpu_custom_call" | custom-call | bytes 14680064 | tf_op jit(solution)/shard_map/pallas_call | solution.py:327
  93.6 2.0 reshape.96.w_dec
  96.3 8.6 %shard_map.194.attended = bf16[2,512,512]{2,1,0:T(8,128)(2,1)} custom-call(bf16[2,512,1536]{2,1,0:T(8,128)(2,1)} %get-tuple-element.105.qkv, bf16[2,32,1024]{2,1,0:T(8,128)(2,1)} %copy-done.41, bf16[2,32,1024]{2,1,0:T(8,128)(2,1)} %collective-permute-done.18.after, f32[576,512]{1,0:T(8,128)} %get-tuple-element.108.log_c), custom_call_target="tpu_custom_call" | custom-call | flops 2147483648 | bytes 8388608 | tf_op jit(solution)/shard_map/pallas_call | solution.py:465
  104.9 31.4 %shard_map.196 = (f32[2,512,512]{2,1,0:T(8,128)}, f32[512,84]{1,0:T(8,128)}, f32[8,512]{1,0:T(8,128)}, f32[1,512]{1,0:T(1,128)}, f32[9984,128]{1,0:T(8,128)}, /*index=5*/f32[9984,128]{1,0:T(8,128)}) custom-call(s32[1]{0:T(128)} %bitcast.refs_0_.me, f32[2,512,512]{2,1,0:T(8,128)} %get-tuple-element.104.h0, bf16[2,512,512]{2,1,0:T(8,128)(2,1)} %shard_map.194.attended, ...), custom_call_target="tpu_custom_call" | custom-call | flops 17179869184 | bytes 25165824 | tf_op jit(solution)/shard_map/pallas_call | solution.py:841
  136.4 17.9 %shard_map.197 = (bf16[2,512,1536]{2,1,0:T(8,128)(2,1)}, f32[2,2,32,1024]{3,2,1,0:T(8,128)}, bf16[2,32,1024]{2,1,0:T(8,128)(2,1)}, bf16[2,32,1024]{2,1,0:T(8,128)(2,1)}) custom-call(bf16[2,512,1536]{2,1,0:T(8,128)(2,1)} %get-tuple-element.105.qkv, bf16[2,32,1024]{2,1,0:T(8,128)(2,1)} %copy-done.41, bf16[2,32,1024]{2,1,0:T(8,128)(2,1)} %collective-permute-done.18.after, ...), custom_call_target="tpu_custom_call" | custom-call | flops 8589934592 | bytes 20971520 | tf_op jit(solution)/shard_map/pallas_call | solution.py:930
  154.4 2.3 collective-permute-start.21
  156.7 1.8 reshape.99.d_dec
  158.5 3.8 %shard_map.198 = (bf16[6,416,128]{2,1,0:T(8,128)(2,1)}, bf16[6,416,128]{2,1,0:T(8,128)(2,1)}) custom-call(f32[24,416,128]{2,1,0:T(8,128)} %bitcast.80, f32[24,416,128]{2,1,0:T(8,128)} %bitcast.12.refs_1_), custom_call_target="tpu_custom_call" | custom-call | bytes 7667712 | tf_op jit(solution)/shard_map/pallas_call | solution.py:611
  163.1 2.8 %collective-permute-start.23 = (bf16[6,416,128]{2,1,0:T(8,128)(2,1)}, bf16[6,416,128]{2,1,0:T(8,128)(2,1)S(1)}, u32[]{:S(2)}, u32[]{:S(2)}) collective-permute-start(bf16[6,416,128]{2,1,0:T(8,128)(2,1)} %get-tuple-element.133), channel_id=1, source_target_pairs={{0,4},{1,5},{2,6},{3,7},{4,0},{5,1},{6,2},{7,3},{8,12},{9,13},{10,... | collective-permute-start | bytes 1916936 | tf_op jit(solution)/shard_map/ppermute | solution.py:346
  166.6 11.1 %shard_map.199 = (bf16[2,512,1024]{2,1,0:T(8,128)(2,1)}, f32[4448,128]{1,0:T(8,128)}, f32[4448,128]{1,0:T(8,128)}) custom-call(s32[1]{0:T(128)} %bitcast.refs_0_.me, bf16[512,1536]{1,0:T(8,128)(2,1)} %get-tuple-element.102.w_qkv, f32[8,512]{1,0:T(8,128)} %get-tuple-element.103.gains, f32[2,512,512]{2,1,0:T(8,128)} %get-tuple-element.104.h0, ...), custom_call_target="tpu_custom_call" | custom-call | flops 8589934592 | bytes 16777216 | tf_op jit(solution)/shard_map/pallas_call | solution.py:995
  177.6 1.4 collective-permute-done.22.refs_2_
  179.1 1.5 collective-permute-done.23.refs_3_
  181.4 5.3 %shard_map.200 = (f32[3,416,128]{2,1,0:T(8,128)}, bf16[3,416,128]{2,1,0:T(8,128)(2,1)}, f32[3,416,128]{2,1,0:T(8,128)}, bf16[3,416,128]{2,1,0:T(8,128)(2,1)}) custom-call(f32[24,416,128]{2,1,0:T(8,128)} %bitcast.81, f32[24,416,128]{2,1,0:T(8,128)} %bitcast.12.refs_1_, bf16[6,416,128]{2,1,0:T(8,128)(2,1)} %copy-done.26, bf16[6,416,128]{2,1,0:T(8,128)(2,1)} %copy-done.27), custom_call_target="tpu_custom_call" | custom-call | bytes 7667712 | tf_op jit(solution)/shard_map/pallas_call | solution.py:611
  186.7 1.8 collective-permute-start.24
  188.5 1.4 collective-permute-start.25
  189.9 13.0 %shard_map.201 = (f32[4448,128]{1,0:T(8,128)}, f32[4448,128]{1,0:T(8,128)}) custom-call(s32[1]{0:T(128)} %bitcast.refs_0_.me, bf16[2,264,2048]{2,1,0:T(8,128)(2,1)} %bitcast.98, bf16[264,512]{1,0:T(8,128)(2,1)} %get-tuple-element.100.w_enc, bf16[2048,512]{1,0:T(8,128)(2,1)} %get-tuple-element.121.enc_mt, ...), custom_call_target="tpu_custom_call", output_to_operand_aliasing={{0}: (5, {}), {1}: (6, {})} | custom-call | flops 8589934592 | bytes 12582912 | tf_op jit(solution)/shard_map/pallas_call | solution.py:1042
  207.8 1.9 add.146
  211.3 3.9 %collective-permute-start.34 = (bf16[832,128]{1,0:T(8,128)(2,1)S(1)}, bf16[832,128]{1,0:T(8,128)(2,1)S(1)}, u32[]{:S(2)}, u32[]{:S(2)}) collective-permute-start(bf16[832,128]{1,0:T(8,128)(2,1)S(1)} %pad_maximum_fusion.9), channel_id=1, source_target_pairs={{0,8},{1,9},{2,10},{3,11},{4,12},{5,13},{6,14},{7,15},{16,24},{17,... | collective-permute-start | bytes 638984 | tf_op jit(solution)/shard_map/ppermute | solution.py:576
  215.2 2.9 %collective-permute-start.35 = (bf16[832,128]{1,0:T(8,128)(2,1)S(1)}, bf16[832,128]{1,0:T(8,128)(2,1)S(1)}, u32[]{:S(2)}, u32[]{:S(2)}) collective-permute-start(bf16[832,128]{1,0:T(8,128)(2,1)S(1)} %pad_maximum_fusion.10), channel_id=1, source_target_pairs={{0,16},{1,17},{2,18},{3,19},{4,20},{5,21},{6,22},{7,23},{8,24},{9,... | collective-permute-start | bytes 638984 | tf_op jit(solution)/shard_map/ppermute | solution.py:576
  218.0 2.7 %collective-permute-done.29 = bf16[1392,128]{1,0:T(8,128)(2,1)S(1)} collective-permute-done((bf16[1392,128]{1,0:T(8,128)(2,1)S(1)}, bf16[1392,128]{1,0:T(8,128)(2,1)S(1)}, u32[]{:S(2)}, u32[]{:S(2)}) %collective-permute-start.29) | collective-permute-done | bytes 356384 | tf_op jit(solution)/shard_map/ppermute | solution.py:346
  221.3 1.8 collective-permute-start.28
  223.8 2.7 %collective-permute-start.36 = (bf16[832,128]{1,0:T(8,128)(2,1)S(1)}, bf16[832,128]{1,0:T(8,128)(2,1)S(1)}, u32[]{:S(2)}, u32[]{:S(2)}) collective-permute-start(bf16[832,128]{1,0:T(8,128)(2,1)S(1)} %pad_maximum_fusion.11), channel_id=1, source_target_pairs={{0,24},{1,25},{2,26},{3,27},{4,28},{5,29},{6,30},{7,31},{8,16},{9,... | collective-permute-start | bytes 638984 | tf_op jit(solution)/shard_map/ppermute | solution.py:576
  226.6 2.3 collective-permute-done.28
  231.3 3.7 %collective-permute-start.31 = (bf16[832,128]{1,0:T(8,128)(2,1)S(1)}, bf16[832,128]{1,0:T(8,128)(2,1)S(1)}, u32[]{:S(2)}, u32[]{:S(2)}) collective-permute-start(bf16[832,128]{1,0:T(8,128)(2,1)S(1)} %get-tuple-element.173), channel_id=1, source_target_pairs={{0,8},{8,0},{9,1},{10,2},{11,3},{12,4},{13,5},{14,6},{15,7},{23,31}} | collective-permute-start | bytes 638984 | tf_op jit(solution)/shard_map/ppermute | solution.py:576
  237.7 5.5 %collective-permute-done.31 = bf16[832,128]{1,0:T(8,128)(2,1)S(1)} collective-permute-done((bf16[832,128]{1,0:T(8,128)(2,1)S(1)}, bf16[832,128]{1,0:T(8,128)(2,1)S(1)}, u32[]{:S(2)}, u32[]{:S(2)}) %collective-permute-start.31) | collective-permute-done | bytes 213024 | tf_op jit(solution)/shard_map/ppermute | solution.py:576
  243.2 4.8 %collective-permute-done.32 = bf16[832,128]{1,0:T(8,128)(2,1)S(1)} collective-permute-done((bf16[832,128]{1,0:T(8,128)(2,1)S(1)}, bf16[832,128]{1,0:T(8,128)(2,1)S(1)}, u32[]{:S(2)}, u32[]{:S(2)}) %collective-permute-start.32) | collective-permute-done | bytes 213024 | tf_op jit(solution)/shard_map/ppermute | solution.py:576
  251.4 3.2 %collective-permute-done.38 = f32[2,8]{1,0:T(2,128)S(1)} collective-permute-done((f32[2,8]{1,0:T(2,128)S(1)}, f32[2,8]{1,0:T(2,128)S(1)}, u32[]{:S(2)}, u32[]{:S(2)}) %collective-permute-start.38) | collective-permute-done | bytes 96 | tf_op jit(solution)/shard_map/ppermute | solution.py:346
  255.2 3.1 %collective-permute-done.39 = f32[2,8]{1,0:T(2,128)S(1)} collective-permute-done((f32[2,8]{1,0:T(2,128)S(1)}, f32[2,8]{1,0:T(2,128)S(1)}, u32[]{:S(2)}, u32[]{:S(2)}) %collective-permute-start.39) | collective-permute-done | bytes 96 | tf_op jit(solution)/shard_map/ppermute | solution.py:346
  258.3 2.8 %collective-permute-start.40 = (f32[2,8]{1,0:T(2,128)S(1)}, f32[2,8]{1,0:T(2,128)S(1)}, u32[]{:S(2)}, u32[]{:S(2)}) collective-permute-start(f32[2,8]{1,0:T(2,128)S(1)} %add.175), channel_id=1, source_target_pairs={{0,8},{1,9},{2,10},{3,11},{4,12},{5,13},{6,14},{7,15},{8,0},{9,1},... | collective-permute-start | bytes 200 | tf_op jit(solution)/shard_map/ppermute | solution.py:346
  261.2 1.5 collective-permute-done.40
  263.7 3.5 %collective-permute-done.41 = f32[2,8]{1,0:T(2,128)S(1)} collective-permute-done((f32[2,8]{1,0:T(2,128)S(1)}, f32[2,8]{1,0:T(2,128)S(1)}, u32[]{:S(2)}, u32[]{:S(2)}) %collective-permute-start.41) | collective-permute-done | bytes 96 | tf_op jit(solution)/shard_map/ppermute | solution.py:346
  (217 shorter events, 36.9 us)
Async XLA Ops:
  7.9 26.8 %copy-start.43 = (f32[84]{0:T(128)S(1)}, f32[84]{0:T(128)}, u32[]{:S(2)}) copy-start(f32[84]{0:T(128)} %param.19) | copy-start | bytes 1012
  7.9 27.4 %copy-start.31 = (s32[2,2048]{1,0:T(2,128)S(1)}, s32[2,2048]{1,0:T(2,128)}, u32[]{:S(2)}) copy-start(s32[2,2048]{1,0:T(2,128)} %param.20) | copy-start | bytes 49156
  7.9 27.4 %copy-start.32 = (f32[2048]{0:T(1024)S(1)}, f32[2048]{0:T(1024)}, u32[]{:S(2)}) copy-start(f32[2048]{0:T(1024)} %param.17) | copy-start | bytes 24580
  7.9 27.4 %copy-start.40 = (f32[2]{0:T(128)S(1)}, f32[2]{0:T(128)}, u32[]{:S(2)}) copy-start(f32[2]{0:T(128)} %param.18) | copy-start | bytes 28
  8.3 31.3 %copy-start.13 = (bf16[224,512]{1,0:T(8,128)(2,1)}, bf16[224,512]{1,0:T(8,128)(2,1)S(1)}, u32[]{:S(2)}) copy-start(bf16[224,512]{1,0:T(8,128)(2,1)S(1)} %reshape.94.refs_1_) | copy-start | bytes 688132
  8.3 18.2 %collective-permute-start.1 = (bf16[224,512]{1,0:T(8,128)(2,1)S(1)}, bf16[224,512]{1,0:T(8,128)(2,1)S(1)}, u32[]{:S(2)}, u32[]{:S(2)}) collective-permute-start(bf16[224,512]{1,0:T(8,128)(2,1)S(1)} %reshape.94.refs_1_), channel_id=1, source_target_pairs={{0,8},{1,9},{2,10},{3,11},{4,12},{5,13},{6,14},{7,15},{8,0},{9,1},... | collective-permute-start | bytes 688136 | tf_op jit(solution)/shard_map/ppermute | solution.py:346
  11.4 19.3 %collective-permute-start.2 = (bf16[224,512]{1,0:T(8,128)(2,1)S(1)}, bf16[224,512]{1,0:T(8,128)(2,1)S(1)}, u32[]{:S(2)}, u32[]{:S(2)}) collective-permute-start(bf16[224,512]{1,0:T(8,128)(2,1)S(1)} %reshape.94.refs_1_), channel_id=1, source_target_pairs={{0,16},{1,17},{2,18},{3,19},{4,20},{5,21},{6,22},{7,23},{8,24},{9,... | collective-permute-start | bytes 688136 | tf_op jit(solution)/shard_map/ppermute | solution.py:346
  14.0 16.7 %collective-permute-start.3 = (bf16[224,512]{1,0:T(8,128)(2,1)S(1)}, bf16[224,512]{1,0:T(8,128)(2,1)S(1)}, u32[]{:S(2)}, u32[]{:S(2)}) collective-permute-start(bf16[224,512]{1,0:T(8,128)(2,1)S(1)} %reshape.94.refs_1_), channel_id=1, source_target_pairs={{0,24},{1,25},{2,26},{3,27},{4,28},{5,29},{6,30},{7,31},{8,16},{9,... | collective-permute-start | bytes 688136 | tf_op jit(solution)/shard_map/ppermute | solution.py:346
  14.0 16.7 %collective-permute-start.4 = (bf16[224,512]{1,0:T(8,128)(2,1)S(1)}, bf16[224,512]{1,0:T(8,128)(2,1)S(1)}, u32[]{:S(2)}, u32[]{:S(2)}) collective-permute-start(bf16[224,512]{1,0:T(8,128)(2,1)S(1)} %reshape.94.refs_1_), channel_id=1, source_target_pairs={{0,2},{1,3},{2,0},{3,1},{4,6},{5,7},{6,4},{7,5},{8,10},{9,11},{10,... | collective-permute-start | bytes 688136 | tf_op jit(solution)/shard_map/ppermute | solution.py:346
  15.7 15.0 %collective-permute-start.5 = (bf16[224,512]{1,0:T(8,128)(2,1)S(1)}, bf16[224,512]{1,0:T(8,128)(2,1)S(1)}, u32[]{:S(2)}, u32[]{:S(2)}) collective-permute-start(bf16[224,512]{1,0:T(8,128)(2,1)S(1)} %reshape.94.refs_1_), channel_id=1, source_target_pairs={{0,4},{1,5},{2,6},{3,7},{4,0},{5,1},{6,2},{7,3},{8,12},{9,13},{10,... | collective-permute-start | bytes 688136 | tf_op jit(solution)/shard_map/ppermute | solution.py:346
  26.5 24.6 %collective-permute-start = (bf16[224,512]{1,0:T(8,128)(2,1)S(1)}, bf16[224,512]{1,0:T(8,128)(2,1)}, u32[]{:S(2)}, u32[]{:S(2)}) collective-permute-start(bf16[224,512]{1,0:T(8,128)(2,1)S(1)} %reshape.94.refs_1_), channel_id=1, source_target_pairs={{0,1},{1,0},{2,3},{3,2},{4,5},{5,4},{6,7},{7,6},{8,9},{9,8},{10,11... | collective-permute-start | bytes 688136 | tf_op jit(solution)/shard_map/ppermute | solution.py:346
  30.7 17.6 %collective-permute-start.10 = (bf16[672,512]{1,0:T(8,128)(2,1)S(1)}, bf16[672,512]{1,0:T(8,128)(2,1)S(1)}, u32[]{:S(2)}, u32[]{:S(2)}) collective-permute-start(bf16[672,512]{1,0:T(8,128)(2,1)S(1)} %pad_maximum_fusion.1.refs_7_), channel_id=1, source_target_pairs={{0,4},{1,5},{2,6},{3,7},{4,0},{5,1},{6,2},{7,3},{8,12},{9,13},{10,... | collective-permute-start | bytes 2064392 | tf_op jit(solution)/shard_map/ppermute | solution.py:346
  32.3 16.0 %collective-permute-start.9 = (bf16[672,512]{1,0:T(8,128)(2,1)S(1)}, bf16[672,512]{1,0:T(8,128)(2,1)S(1)}, u32[]{:S(2)}, u32[]{:S(2)}) collective-permute-start(bf16[672,512]{1,0:T(8,128)(2,1)S(1)} %pad_maximum_fusion.1.refs_7_), channel_id=1, source_target_pairs={{0,2},{1,3},{2,0},{3,1},{4,6},{5,7},{6,4},{7,5},{8,10},{9,11},{10,... | collective-permute-start | bytes 2064392 | tf_op jit(solution)/shard_map/ppermute | solution.py:346
  48.4 9.3 %collective-permute-start.14 = (bf16[448,512]{1,0:T(8,128)(2,1)S(1)}, bf16[448,512]{1,0:T(8,128)(2,1)S(1)}, u32[]{:S(2)}, u32[]{:S(2)}) collective-permute-start(bf16[448,512]{1,0:T(8,128)(2,1)S(1)} %pad_maximum_fusion.3), channel_id=1, source_target_pairs={{0,4},{1,5},{2,6},{3,7},{4,0},{5,1},{6,2},{7,3},{8,12},{9,13},{10,... | collective-permute-start | bytes 1376264 | tf_op jit(solution)/shard_map/ppermute | solution.py:346
  49.4 9.3 %collective-permute-start.13 = (bf16[448,512]{1,0:T(8,128)(2,1)S(1)}, bf16[448,512]{1,0:T(8,128)(2,1)S(1)}, u32[]{:S(2)}, u32[]{:S(2)}) collective-permute-start(bf16[448,512]{1,0:T(8,128)(2,1)S(1)} %pad_maximum_fusion.2), channel_id=1, source_target_pairs={{0,2},{1,3},{2,0},{3,1},{4,6},{5,7},{6,4},{7,5},{8,10},{9,11},{10,... | collective-permute-start | bytes 1376264 | tf_op jit(solution)/shard_map/ppermute | solution.py:346
  50.5 10.4 %collective-permute-start.8 = (bf16[672,512]{1,0:T(8,128)(2,1)S(1)}, bf16[672,512]{1,0:T(8,128)(2,1)S(1)}, u32[]{:S(2)}, u32[]{:S(2)}) collective-permute-start(bf16[672,512]{1,0:T(8,128)(2,1)S(1)} %copy-done.3), channel_id=1, source_target_pairs={{0,1},{1,0},{2,3},{3,2},{4,5},{5,4},{6,7},{7,6},{8,9},{9,8},{10,11... | collective-permute-start | bytes 2064392 | tf_op jit(solution)/shard_map/ppermute | solution.py:346
  50.6 9.7 %collective-permute-start.6 = (bf16[224,512]{1,0:T(8,128)(2,1)S(1)}, bf16[224,512]{1,0:T(8,128)(2,1)S(1)}, u32[]{:S(2)}, u32[]{:S(2)}) collective-permute-start(bf16[224,512]{1,0:T(8,128)(2,1)S(1)} %copy-done.21), channel_id=1, source_target_pairs={{0,1},{1,0},{2,3},{3,2},{4,5},{5,4},{6,7},{7,6},{8,9},{9,8},{10,11... | collective-permute-start | bytes 688136 | tf_op jit(solution)/shard_map/ppermute | solution.py:346
  51.2 9.7 %collective-permute-start.7 = (bf16[224,512]{1,0:T(8,128)(2,1)S(1)}, bf16[224,512]{1,0:T(8,128)(2,1)S(1)}, u32[]{:S(2)}, u32[]{:S(2)}) collective-permute-start(bf16[224,512]{1,0:T(8,128)(2,1)S(1)} %copy-done.23), channel_id=1, source_target_pairs={{0,1},{1,0},{2,3},{3,2},{4,5},{5,4},{6,7},{7,6},{8,9},{9,8},{10,11... | collective-permute-start | bytes 688136 | tf_op jit(solution)/shard_map/ppermute | solution.py:346
  57.7 3.2 %collective-permute-start.11 = (bf16[672,512]{1,0:T(8,128)(2,1)S(1)}, bf16[672,512]{1,0:T(8,128)(2,1)S(1)}, u32[]{:S(2)}, u32[]{:S(2)}) collective-permute-start(bf16[672,512]{1,0:T(8,128)(2,1)S(1)} %copy-done.7), channel_id=1, source_target_pairs={{0,1},{1,0},{2,3},{3,2},{4,5},{5,4},{6,7},{7,6},{8,9},{9,8},{10,11... | collective-permute-start | bytes 2064392 | tf_op jit(solution)/shard_map/ppermute | solution.py:346
  58.7 2.2 collective-permute-start.12
  60.3 1.9 collective-permute-start.15
  60.8 2.1 collective-permute-start.16
  81.1 14.6 %collective-permute-start.17 = (bf16[2,32,1024]{2,1,0:T(8,128)(2,1)}, bf16[2,32,1024]{2,1,0:T(8,128)(2,1)S(1)}, u32[]{:S(2)}, u32[]{:S(2)}) collective-permute-start(bf16[2,32,1024]{2,1,0:T(8,128)(2,1)} %get-tuple-element.106), channel_id=1, source_target_pairs={{0,4},{4,8},{8,12},{12,16},{16,20},{20,24},{24,28},{28,0},{1,5},{5... | collective-permute-start | bytes 393224 | tf_op jit(solution)/shard_map/ppermute | solution.py:1127
  82.0 13.6 %collective-permute-start.18 = (bf16[2,32,1024]{2,1,0:T(8,128)(2,1)}, bf16[2,32,1024]{2,1,0:T(8,128)(2,1)}, u32[]{:S(2)}, u32[]{:S(2)}) collective-permute-start(bf16[2,32,1024]{2,1,0:T(8,128)(2,1)} %get-tuple-element.107), channel_id=1, source_target_pairs={{0,28},{4,0},{8,4},{12,8},{16,12},{20,16},{24,20},{28,24},{1,29},{... | collective-permute-start | bytes 393224 | tf_op jit(solution)/shard_map/ppermute | solution.py:1128
  136.3 18.0 %collective-permute-start.19 = (f32[9984,128]{1,0:T(8,128)}, f32[9984,128]{1,0:T(8,128)}, u32[]{:S(2)}, u32[]{:S(2)}) collective-permute-start(f32[9984,128]{1,0:T(8,128)} %get-tuple-element.123), channel_id=1, source_target_pairs={{0,1},{1,0},{2,3},{3,2},{4,5},{5,4},{6,7},{7,6},{8,9},{9,8},{10,11... | collective-permute-start | bytes 15335432 | tf_op jit(solution)/shard_map/ppermute | solution.py:346
  154.2 11.7 %collective-permute-start.20 = (bf16[2,32,1024]{2,1,0:T(8,128)(2,1)}, bf16[2,32,1024]{2,1,0:T(8,128)(2,1)S(1)}, u32[]{:S(2)}, u32[]{:S(2)}) collective-permute-start(bf16[2,32,1024]{2,1,0:T(8,128)(2,1)} %get-tuple-element.135), channel_id=1, source_target_pairs={{0,28},{4,0},{8,4},{12,8},{16,12},{20,16},{24,20},{28,24},{1,29},{... | collective-permute-start | bytes 393224 | tf_op jit(solution)/shard_map/ppermute | solution.py:1143
  154.4 11.5 %collective-permute-start.21 = (bf16[2,32,1024]{2,1,0:T(8,128)(2,1)}, bf16[2,32,1024]{2,1,0:T(8,128)(2,1)}, u32[]{:S(2)}, u32[]{:S(2)}) collective-permute-start(bf16[2,32,1024]{2,1,0:T(8,128)(2,1)} %get-tuple-element.136), channel_id=1, source_target_pairs={{0,4},{4,8},{8,12},{12,16},{16,20},{20,24},{24,28},{28,0},{1,5},{5... | collective-permute-start | bytes 393224 | tf_op jit(solution)/shard_map/ppermute | solution.py:1144
  162.3 16.7 %collective-permute-start.22 = (bf16[6,416,128]{2,1,0:T(8,128)(2,1)}, bf16[6,416,128]{2,1,0:T(8,128)(2,1)S(1)}, u32[]{:S(2)}, u32[]{:S(2)}) collective-permute-start(bf16[6,416,128]{2,1,0:T(8,128)(2,1)} %get-tuple-element.132), channel_id=1, source_target_pairs={{0,2},{1,3},{2,0},{3,1},{4,6},{5,7},{6,4},{7,5},{8,10},{9,11},{10,... | collective-permute-start | bytes 1916936 | tf_op jit(solution)/shard_map/ppermute | solution.py:346
  163.1 17.5 %collective-permute-start.23 = (bf16[6,416,128]{2,1,0:T(8,128)(2,1)}, bf16[6,416,128]{2,1,0:T(8,128)(2,1)S(1)}, u32[]{:S(2)}, u32[]{:S(2)}) collective-permute-start(bf16[6,416,128]{2,1,0:T(8,128)(2,1)} %get-tuple-element.133), channel_id=1, source_target_pairs={{0,4},{1,5},{2,6},{3,7},{4,0},{5,1},{6,2},{7,3},{8,12},{9,13},{10,... | collective-permute-start | bytes 1916936 | tf_op jit(solution)/shard_map/ppermute | solution.py:346
  186.7 16.3 %collective-permute-start.24 = (bf16[3,416,128]{2,1,0:T(8,128)(2,1)}, bf16[3,416,128]{2,1,0:T(8,128)(2,1)}, u32[]{:S(2)}, u32[]{:S(2)}) collective-permute-start(bf16[3,416,128]{2,1,0:T(8,128)(2,1)} %get-tuple-element.149), channel_id=1, source_target_pairs={{0,4},{1,5},{2,6},{3,7},{4,0},{5,1},{6,2},{7,3},{8,12},{9,13},{10,... | collective-permute-start | bytes 958472 | tf_op jit(solution)/shard_map/ppermute | solution.py:346
  188.5 14.5 %collective-permute-start.25 = (bf16[3,416,128]{2,1,0:T(8,128)(2,1)}, bf16[3,416,128]{2,1,0:T(8,128)(2,1)}, u32[]{:S(2)}, u32[]{:S(2)}) collective-permute-start(bf16[3,416,128]{2,1,0:T(8,128)(2,1)} %get-tuple-element.150), channel_id=1, source_target_pairs={{0,2},{1,3},{2,0},{3,1},{4,6},{5,7},{6,4},{7,5},{8,10},{9,11},{10,... | collective-permute-start | bytes 958472 | tf_op jit(solution)/shard_map/ppermute | solution.py:346
  203.0 4.8 %collective-permute-start.26 = (f32[4448,128]{1,0:T(8,128)}, f32[4448,128]{1,0:T(8,128)}, u32[]{:S(2)}, u32[]{:S(2)}) collective-permute-start(f32[4448,128]{1,0:T(8,128)} %get-tuple-element.157), channel_id=1, source_target_pairs={{0,1},{1,0},{2,3},{3,2},{4,5},{5,4},{6,7},{7,6},{8,9},{9,8},{10,11... | collective-permute-start | bytes 6832136 | tf_op jit(solution)/shard_map/ppermute | solution.py:346
  210.0 10.7 %collective-permute-start.29 = (bf16[1392,128]{1,0:T(8,128)(2,1)S(1)}, bf16[1392,128]{1,0:T(8,128)(2,1)S(1)}, u32[]{:S(2)}, u32[]{:S(2)}) collective-permute-start(bf16[1392,128]{1,0:T(8,128)(2,1)S(1)} %pad_maximum_fusion.6), channel_id=1, source_target_pairs={{0,4},{1,5},{2,6},{3,7},{4,0},{5,1},{6,2},{7,3},{8,12},{9,13},{10,... | collective-permute-start | bytes 1069064 | tf_op jit(solution)/shard_map/ppermute | solution.py:346
  210.5 10.4 %collective-permute-start.27 = (bf16[1392,128]{1,0:T(8,128)(2,1)S(1)}, bf16[1392,128]{1,0:T(8,128)(2,1)S(1)}, u32[]{:S(2)}, u32[]{:S(2)}) collective-permute-start(bf16[1392,128]{1,0:T(8,128)(2,1)S(1)} %pad_maximum_fusion.5), channel_id=1, source_target_pairs={{0,2},{1,3},{2,0},{3,1},{4,6},{5,7},{6,4},{7,5},{8,10},{9,11},{10,... | collective-permute-start | bytes 1069064 | tf_op jit(solution)/shard_map/ppermute | solution.py:346
  211.3 25.1 %collective-permute-start.34 = (bf16[832,128]{1,0:T(8,128)(2,1)S(1)}, bf16[832,128]{1,0:T(8,128)(2,1)S(1)}, u32[]{:S(2)}, u32[]{:S(2)}) collective-permute-start(bf16[832,128]{1,0:T(8,128)(2,1)S(1)} %pad_maximum_fusion.9), channel_id=1, source_target_pairs={{0,8},{1,9},{2,10},{3,11},{4,12},{5,13},{6,14},{7,15},{16,24},{17,... | collective-permute-start | bytes 638984 | tf_op jit(solution)/shard_map/ppermute | solution.py:576
  215.2 22.5 %collective-permute-start.35 = (bf16[832,128]{1,0:T(8,128)(2,1)S(1)}, bf16[832,128]{1,0:T(8,128)(2,1)S(1)}, u32[]{:S(2)}, u32[]{:S(2)}) collective-permute-start(bf16[832,128]{1,0:T(8,128)(2,1)S(1)} %pad_maximum_fusion.10), channel_id=1, source_target_pairs={{0,16},{1,17},{2,18},{3,19},{4,20},{5,21},{6,22},{7,23},{8,24},{9,... | collective-permute-start | bytes 638984 | tf_op jit(solution)/shard_map/ppermute | solution.py:576
  221.3 7.6 %collective-permute-start.28 = (bf16[976,128]{1,0:T(8,128)(2,1)S(1)}, bf16[976,128]{1,0:T(8,128)(2,1)S(1)}, u32[]{:S(2)}, u32[]{:S(2)}) collective-permute-start(bf16[976,128]{1,0:T(8,128)(2,1)S(1)} %pad_maximum_fusion.7), channel_id=1, source_target_pairs={{0,4},{1,5},{2,6},{3,7},{4,0},{5,1},{6,2},{7,3},{8,12},{9,13},{10,... | collective-permute-start | bytes 749576 | tf_op jit(solution)/shard_map/ppermute | solution.py:346
  223.1 7.1 %collective-permute-start.30 = (bf16[976,128]{1,0:T(8,128)(2,1)S(1)}, bf16[976,128]{1,0:T(8,128)(2,1)S(1)}, u32[]{:S(2)}, u32[]{:S(2)}) collective-permute-start(bf16[976,128]{1,0:T(8,128)(2,1)S(1)} %pad_maximum_fusion.8), channel_id=1, source_target_pairs={{0,2},{1,3},{2,0},{3,1},{4,6},{5,7},{6,4},{7,5},{8,10},{9,11},{10,... | collective-permute-start | bytes 749576 | tf_op jit(solution)/shard_map/ppermute | solution.py:346
  223.8 13.9 %collective-permute-start.36 = (bf16[832,128]{1,0:T(8,128)(2,1)S(1)}, bf16[832,128]{1,0:T(8,128)(2,1)S(1)}, u32[]{:S(2)}, u32[]{:S(2)}) collective-permute-start(bf16[832,128]{1,0:T(8,128)(2,1)S(1)} %pad_maximum_fusion.11), channel_id=1, source_target_pairs={{0,24},{1,25},{2,26},{3,27},{4,28},{5,29},{6,30},{7,31},{8,16},{9,... | collective-permute-start | bytes 638984 | tf_op jit(solution)/shard_map/ppermute | solution.py:576
  231.3 11.9 %collective-permute-start.31 = (bf16[832,128]{1,0:T(8,128)(2,1)S(1)}, bf16[832,128]{1,0:T(8,128)(2,1)S(1)}, u32[]{:S(2)}, u32[]{:S(2)}) collective-permute-start(bf16[832,128]{1,0:T(8,128)(2,1)S(1)} %get-tuple-element.173), channel_id=1, source_target_pairs={{0,8},{8,0},{9,1},{10,2},{11,3},{12,4},{13,5},{14,6},{15,7},{23,31}} | collective-permute-start | bytes 638984 | tf_op jit(solution)/shard_map/ppermute | solution.py:576
  235.0 13.0 %collective-permute-start.32 = (bf16[832,128]{1,0:T(8,128)(2,1)S(1)}, bf16[832,128]{1,0:T(8,128)(2,1)S(1)}, u32[]{:S(2)}, u32[]{:S(2)}) collective-permute-start(bf16[832,128]{1,0:T(8,128)(2,1)S(1)} %get-tuple-element.175), channel_id=1, source_target_pairs={{15,31},{16,0},{17,1},{18,2},{19,3},{20,4},{21,5},{22,6},{23,7},{2... | collective-permute-start | bytes 638984 | tf_op jit(solution)/shard_map/ppermute | solution.py:576
  236.3 11.7 %collective-permute-start.33 = (bf16[832,128]{1,0:T(8,128)(2,1)S(1)}, bf16[832,128]{1,0:T(8,128)(2,1)S(1)}, u32[]{:S(2)}, u32[]{:S(2)}) collective-permute-start(bf16[832,128]{1,0:T(8,128)(2,1)S(1)} %get-tuple-element.174), channel_id=1, source_target_pairs={{7,31},{16,8},{24,0},{25,1},{26,2},{27,3},{28,4},{29,5},{30,6},{31... | collective-permute-start | bytes 638984 | tf_op jit(solution)/shard_map/ppermute | solution.py:576
  248.7 20.3 %copy-start.18 = (f32[103920]{0:T(1024)}, f32[103920]{0:T(1024)S(1)}, u32[]{:S(2)}) copy-start(f32[103920]{0:T(1024)S(1)} %get-tuple-element.165) | copy-start | bytes 1247044
  249.9 1.2 collective-permute-start.37
  251.1 3.6 %collective-permute-start.38 = (f32[2,8]{1,0:T(2,128)S(1)}, f32[2,8]{1,0:T(2,128)S(1)}, u32[]{:S(2)}, u32[]{:S(2)}) collective-permute-start(f32[2,8]{1,0:T(2,128)S(1)} %fusion.35), channel_id=1, source_target_pairs={{0,2},{1,3},{2,0},{3,1},{4,6},{5,7},{6,4},{7,5},{8,10},{9,11},{10,... | collective-permute-start | bytes 200 | tf_op jit(solution)/shard_map/ppermute | solution.py:346
  254.7 3.6 %collective-permute-start.39 = (f32[2,8]{1,0:T(2,128)S(1)}, f32[2,8]{1,0:T(2,128)S(1)}, u32[]{:S(2)}, u32[]{:S(2)}) collective-permute-start(f32[2,8]{1,0:T(2,128)S(1)} %fusion.36), channel_id=1, source_target_pairs={{0,4},{1,5},{2,6},{3,7},{4,0},{5,1},{6,2},{7,3},{8,12},{9,13},{10,... | collective-permute-start | bytes 200 | tf_op jit(solution)/shard_map/ppermute | solution.py:346
  258.3 4.4 %collective-permute-start.40 = (f32[2,8]{1,0:T(2,128)S(1)}, f32[2,8]{1,0:T(2,128)S(1)}, u32[]{:S(2)}, u32[]{:S(2)}) collective-permute-start(f32[2,8]{1,0:T(2,128)S(1)} %add.175), channel_id=1, source_target_pairs={{0,8},{1,9},{2,10},{3,11},{4,12},{5,13},{6,14},{7,15},{8,0},{9,1},... | collective-permute-start | bytes 200 | tf_op jit(solution)/shard_map/ppermute | solution.py:346
  262.7 4.5 %collective-permute-start.41 = (f32[2,8]{1,0:T(2,128)S(1)}, f32[2,8]{1,0:T(2,128)S(1)}, u32[]{:S(2)}, u32[]{:S(2)}) collective-permute-start(f32[2,8]{1,0:T(2,128)S(1)} %add.176), channel_id=1, source_target_pairs={{0,16},{1,17},{2,18},{3,19},{4,20},{5,21},{6,22},{7,23},{8,24},{9,... | collective-permute-start | bytes 200 | tf_op jit(solution)/shard_map/ppermute | solution.py:346
  (39 other events, 266.3 us)
